TPU v7x, 128 devices: a whole 4x4x4 slice. The times are simulated.
128 devices in a mesh: span: 4 (over z_lo, core), cp: 32 (over y, z_hi, x).
Axes of the slice: x: 4, y: 4, z: 4 (z_hi: 2, z_lo: 2; z = z_hi * 2 + z_lo), core: 2. Of those that a mesh axis runs over, the one named last changes fastest.
Arguments:
- queries: bfloat16 [4, 3072, 4096], P('span', 'cp'), may hold values from -12 to 12
- keys: bfloat16 [4, 3072, 4096], P('span', 'cp'), may hold values from -40 to 40
- values: bfloat16 [4, 3072, 4096], P('span', 'cp'), may hold values from -6 to 6
- cache_keys: bfloat16 [3072, 4096], P('span', 'cp'), may hold values from -10 to 10
- cache_values: bfloat16 [3072, 4096], P('span', 'cp'), may hold values from -6 to 6
- gate_table: float32 [64, 4096], replicated, may hold values from -8 to 8
- noise_steps: int32 [4], replicated, may hold values from 0 to 63
- span_order: int32 [4], replicated, may hold values from 0 to 3, each once
- block_mask: int32 [4, 8], replicated, may hold values 0 or 1
Outputs:
- gated_attention: bfloat16 [4, 3072, 4096], P('span', 'cp')
Inputs may be any that keep to these rules, and one draw needn't show every extreme that they name: `span_order`: each of 0 to 3 once.
All inputs are finite; a program needn't handle non-finite values.
Results may differ from a plain program's by a relative error of at most 0.0055.
Values may be sent and summed in bfloat16 or wider, within the bound.
No kernel may reach another device: no remote copies, remote signals or barrier semaphores. Data moves between devices by JAX's collectives and lax.ppermute only.
A program may use at most 128 MiB of HBM per device.

v0:
```python
import math

import jax
import jax.numpy as jnp
from jax import lax
from jax.sharding import PartitionSpec as P

H = 32
HD = 128
NBLK = 8


def pick_entries(table_vector, indices):
    count = table_vector.shape[0]
    match = indices[:, None] == jnp.arange(count, dtype=jnp.int32)[None, :]
    return jnp.sum(jnp.where(match, table_vector[None, :], 0), axis=1)


def attend(state, query_sets, piece_keys, piece_values, visible):
    maxima, totals, weighted = state
    query_count = query_sets.shape[1]
    block_rows = 512
    blocks = query_count // block_rows
    score_scale = 1.0 / math.sqrt(query_sets.shape[3])
    max_list, total_list, sum_list = ([], [], [])
    mask_row = visible[0]

    def one_block(items):
        query_block, max_block, total_block, sum_block = items
        scores = (
            jnp.einsum("qhd,khd->qhk", query_block, piece_keys, preferred_element_type=jnp.float32)
            * score_scale
        )
        scores = jnp.where(mask_row[None, None, :], scores, -1e30)
        running = jnp.maximum(max_block, jnp.max(scores, axis=2))
        weights = jnp.exp(scores - running[:, :, None])
        rescale = jnp.exp(max_block - running)
        total_block = total_block * rescale + jnp.sum(weights, axis=2)
        sum_block = sum_block * rescale[:, :, None] + jnp.einsum(
            "qhk,khd->qhd",
            weights.astype(jnp.bfloat16),
            piece_values,
            preferred_element_type=jnp.float32,
        )
        return (running, total_block, sum_block)

    def update(member_parts):
        shaped = tuple(
            (
                member_part.reshape((blocks, block_rows) + member_part.shape[1:])
                for member_part in member_parts
            )
        )
        mapped = lax.map(one_block, shaped)
        return tuple((result.reshape((query_count,) + result.shape[2:]) for result in mapped))

    def unchanged(member_parts):
        return (member_parts[1], member_parts[2], member_parts[3])

    new_max, new_total, new_sum = lax.cond(
        jnp.any(mask_row), update, unchanged, (query_sets[0], maxima[0], totals[0], weighted[0])
    )
    max_list.append(new_max)
    total_list.append(new_total)
    sum_list.append(new_sum)
    return (jnp.stack(max_list), jnp.stack(total_list), jnp.stack(sum_list))


def on_device(
    queries, keys, values, cache_keys, cache_values, gate_table, noise_steps, span_order, block_mask
):
    spans = lax.axis_size("span")
    ranks = lax.axis_size("cp")
    local_rows = queries.shape[1]
    width = queries.shape[2]
    per_device = H // ranks
    span_tokens = local_rows * ranks
    group = lax.axis_index("span")
    row_queries = queries.reshape(local_rows, H, HD)
    row_keys = keys.reshape(local_rows, H, HD)
    row_values = values.reshape(local_rows, H, HD)
    head_queries, head_keys, head_values = (
        lax.all_to_all(row_queries, "cp", split_axis=1, concat_axis=0, tiled=True),
        lax.all_to_all(row_keys, "cp", split_axis=1, concat_axis=0, tiled=True),
        lax.all_to_all(row_values, "cp", split_axis=1, concat_axis=0, tiled=True),
    )
    query_sets = head_queries[None]
    query_span = jnp.reshape(group, (1,))
    query_order = pick_entries(span_order, query_span)
    members = query_sets.shape[0]
    query_count = query_sets.shape[1]
    initial = (
        jnp.full((members, query_count, per_device), -1e30, jnp.float32),
        jnp.zeros((members, query_count, per_device), jnp.float32),
        jnp.zeros((members, query_count, per_device, HD), jnp.float32),
    )
    piece_keys = lax.all_gather(head_keys, "span", axis=0, tiled=True)
    piece_values = lax.all_gather(head_values, "span", axis=0, tiled=True)
    count = piece_keys.shape[0]
    key_span = jnp.arange(count, dtype=jnp.int32) // span_tokens
    key_order = pick_entries(span_order, key_span)
    visible = key_order[None, :] <= query_order[:, None]
    state = attend(initial, query_sets, piece_keys, piece_values, visible)
    cache_rows = cache_keys.shape[0]
    local_cache_keys = cache_keys.reshape(cache_rows, per_device, HD)
    local_cache_values = cache_values.reshape(cache_rows, per_device, HD)
    block_tokens = span_tokens // NBLK
    span_match = query_span[:, None] == jnp.arange(spans, dtype=jnp.int32)[None, :]
    mask_rows = jnp.sum(jnp.where(span_match[:, :, None], block_mask[None, :, :], 0), axis=1)
    piece_keys = lax.all_gather(local_cache_keys, "span", axis=0, tiled=True)
    piece_values = lax.all_gather(local_cache_values, "span", axis=0, tiled=True)
    count = piece_keys.shape[0]
    block_index = jnp.arange(count, dtype=jnp.int32) // block_tokens
    block_match = block_index[None, :, None] == jnp.arange(NBLK, dtype=jnp.int32)[None, None, :]
    visible = jnp.sum(jnp.where(block_match, mask_rows[:, None, :], 0), axis=2) > 0
    maxima, totals, weighted = attend(state, query_sets, piece_keys, piece_values, visible)
    attention = (weighted / totals[:, :, :, None]).astype(jnp.bfloat16)
    row_attention = lax.all_to_all(attention[0], "cp", split_axis=0, concat_axis=1, tiled=True)
    step_now = pick_entries(noise_steps, jnp.reshape(group, (1,)))[0]
    level_match = jnp.arange(gate_table.shape[0], dtype=jnp.int32) == step_now
    gate_row = jnp.sum(jnp.where(level_match[:, None], gate_table, 0.0), axis=0)
    gated = (
        row_attention.reshape(local_rows, width).astype(jnp.float32) * gate_row[None, :]
    ).astype(jnp.bfloat16)
    return gated[None]


def solution(mesh):
    placed = (
        P("span", "cp", None),
        P("span", "cp", None),
        P("span", "cp", None),
        P("span", "cp"),
        P("span", "cp"),
        P(),
        P(),
        P(),
        P(),
    )
    return jax.shard_map(
        on_device, mesh=mesh, in_specs=placed, out_specs=P("span", "cp", None), check_vma=False
    )
```

profile of v0, /device:TPU:1, one launch (start us, length us, event | category | flops | bytes accessed | tf_op | source)
XLA Modules:
  0.0 434.9 jit_solution(13405766481001882435)
XLA Ops:
  8.3 25.1 %all_to_all.63 = bf16[96,32,128]{2,0,1:T(8,128)(2,1)} all-to-all(bf16[96,32,128]{2,0,1:T(8,128)(2,1)S(1)} %copy.43), channel_id=1, replica_groups=mesh['span'=4,'cp'=32] {'cp'}, dimensions={1} | all-to-all | bytes 1572864 | tf_op jit(solution)/shard_map/all_to_all | solution.py:84
  35.1 17.4 %all_to_all.64 = bf16[96,32,128]{2,0,1:T(8,128)(2,1)} all-to-all(bf16[96,32,128]{2,0,1:T(8,128)(2,1)S(1)} %copy.44), channel_id=1, replica_groups=mesh['span'=4,'cp'=32] {'cp'}, dimensions={1} | all-to-all | bytes 1572864 | tf_op jit(solution)/shard_map/all_to_all | solution.py:85
  64.3 18.1 %all-gather = bf16[3072,128]{1,0:T(8,128)(2,1)S(1)} all-gather(bf16[768,128]{1,0:T(8,128)(2,1)S(1)} %copy-done.2), channel_id=2, replica_groups=mesh['span'=4,'cp'=32] {'span'}, dimensions={0}, use_global_device_ids=true | all-gather | bytes 983040 | tf_op jit(solution)/shard_map/all_gather | solution.py:110
  82.4 12.6 %all-gather.1 = bf16[3072,128]{1,0:T(8,128)(2,1)S(1)} all-gather(bf16[768,128]{1,0:T(8,128)(2,1)S(1)} %copy-done.3), channel_id=3, replica_groups=mesh['span'=4,'cp'=32] {'span'}, dimensions={0}, use_global_device_ids=true | all-gather | bytes 983040 | tf_op jit(solution)/shard_map/all_gather | solution.py:111
  95.0 38.7 %all-gather.7.cloned.1.call-done = bf16[12288,1,128]{2,0,1:T(8,128)(2,1)} async-done(((bf16[3072,1,128]{2,0,1:T(8,128)(2,1)}), bf16[12288,1,128]{2,0,1:T(8,128)(2,1)}) %all-gather.7.cloned.1.call-update) | async-done | bytes 3145744 | tf_op jit(solution)/shard_map/all_gather | solution.py:98
  133.8 219.2 %conditional.2 = (f32[3072,1]{0,1:T(1,128)}, f32[3072,1]{0,1:T(1,128)}, f32[3072,1,128]{2,0,1:T(8,128)}) conditional(s32[]{:T(128)} %convert_element_type.44, () %tuple.28, (bf16[3072,1,128]{2,0,1:T(8,128)(2,1)S(1)}, s32[]{:T(128)}, s32[12288]{0:T(1024)S(1)}, bf16[12288,1,128]{2,0,1:T(8,128)(2,1)}, bf16[12288,1,128]{2,0,1:T(8,128)(2,1)}) %tuple.91), branch_computations={%region_6.7_spmd, %region_7.12_spmd} | conditional | flops 3290511360 | bytes 94938360 | solution.py:60
  134.4 218.5 %while.24 = (s32[]{:T(128)}, f32[6,512,1]{1,2,0:T(1,128)}, f32[6,512,1]{1,2,0:T(1,128)}, f32[6,512,1,128]{3,1,2,0:T(8,128)}, pred[1,12288]{1,0:T(4,128)(4,1)S(1)...) while((s32[]{:T(128)}, f32[6,512,1]{1,2,0:T(1,128)}, ...), condition=%wide.region_11.11_spmd, body=%wide.region_8.10_spmd.sunk | while | flops 3290499072 | bytes 94852232 | solution.py:54
  134.6 12.2 %fusion.84 = (f32[512]{0:T(512)S(1)}, f32[512,12288]{1,0:T(8,128)}) fusion(pred[12288]{0:T(1024)(128)(4,1)S(1)} %reduce.21, bf16[12288,1,128]{2,0,1:T(8,128)(2,1)} %get-tuple-element.487, bf16[6,512,1,128]{3,1,2,0:T(8,128)(2,1)S(1)} %get-tuple-element.486, s32[]{:T(128)} %get-tuple-element.471), kind=kOutput, calls=%fused_computation.4.clone.1 | convolution fusion | flops 1629486592 | bytes 28456964 | tf_op jit(solution)/shard_map/cond/branch_1_fun/while/body/eval_jaxpr/qhd,khd->qhk/dot_general | solution.py:31
  146.8 11.9 %fusion.86 = f32[6,512,1,128]{3,1,2,0:T(8,128)} fusion(f32[6,512,1,128]{3,1,2,0:T(8,128)} %get-tuple-element.474, s32[]{:T(128)} %get-tuple-element.471, bf16[12288,1,128]{2,0,1:T(8,128)(2,1)S(1)} %copy-done.6, f32[512,12288]{1,0:T(8,128)} %get-tuple-element.419, f32[512]{0:T(512)S(1)} %get-tuple-element.421, pred[12288]{0:T(1024)(128)(4,1)S(1)} %reduce.21, ...), kind=kOutput, calls=%fused_computation.14.clone.1 | convolution fusion | flops 1635844096 | bytes 28590592 | tf_op jit(solution)/shard_map/cond/branch_1_fun/while/body/eval_jaxpr/qhk,khd->qhd/dot_general | solution.py:39
  171.0 12.2 %fusion.84 = (f32[512]{0:T(512)S(1)}, f32[512,12288]{1,0:T(8,128)}) fusion(pred[12288]{0:T(1024)(128)(4,1)S(1)} %reduce.21, bf16[12288,1,128]{2,0,1:T(8,128)(2,1)} %get-tuple-element.487, bf16[6,512,1,128]{3,1,2,0:T(8,128)(2,1)S(1)} %get-tuple-element.486, s32[]{:T(128)} %get-tuple-element.471), kind=kOutput, calls=%fused_computation.4.clone.1 | convolution fusion | flops 1629486592 | bytes 28456964 | tf_op jit(solution)/shard_map/cond/branch_1_fun/while/body/eval_jaxpr/qhd,khd->qhk/dot_general | solution.py:31
  183.2 11.9 %fusion.86 = f32[6,512,1,128]{3,1,2,0:T(8,128)} fusion(f32[6,512,1,128]{3,1,2,0:T(8,128)} %get-tuple-element.474, s32[]{:T(128)} %get-tuple-element.471, bf16[12288,1,128]{2,0,1:T(8,128)(2,1)S(1)} %copy-done.6, f32[512,12288]{1,0:T(8,128)} %get-tuple-element.419, f32[512]{0:T(512)S(1)} %get-tuple-element.421, pred[12288]{0:T(1024)(128)(4,1)S(1)} %reduce.21, ...), kind=kOutput, calls=%fused_computation.14.clone.1 | convolution fusion | flops 1635844096 | bytes 28590592 | tf_op jit(solution)/shard_map/cond/branch_1_fun/while/body/eval_jaxpr/qhk,khd->qhd/dot_general | solution.py:39
  207.4 12.2 %fusion.84 = (f32[512]{0:T(512)S(1)}, f32[512,12288]{1,0:T(8,128)}) fusion(pred[12288]{0:T(1024)(128)(4,1)S(1)} %reduce.21, bf16[12288,1,128]{2,0,1:T(8,128)(2,1)} %get-tuple-element.487, bf16[6,512,1,128]{3,1,2,0:T(8,128)(2,1)S(1)} %get-tuple-element.486, s32[]{:T(128)} %get-tuple-element.471), kind=kOutput, calls=%fused_computation.4.clone.1 | convolution fusion | flops 1629486592 | bytes 28456964 | tf_op jit(solution)/shard_map/cond/branch_1_fun/while/body/eval_jaxpr/qhd,khd->qhk/dot_general | solution.py:31
  219.7 11.9 %fusion.86 = f32[6,512,1,128]{3,1,2,0:T(8,128)} fusion(f32[6,512,1,128]{3,1,2,0:T(8,128)} %get-tuple-element.474, s32[]{:T(128)} %get-tuple-element.471, bf16[12288,1,128]{2,0,1:T(8,128)(2,1)S(1)} %copy-done.6, f32[512,12288]{1,0:T(8,128)} %get-tuple-element.419, f32[512]{0:T(512)S(1)} %get-tuple-element.421, pred[12288]{0:T(1024)(128)(4,1)S(1)} %reduce.21, ...), kind=kOutput, calls=%fused_computation.14.clone.1 | convolution fusion | flops 1635844096 | bytes 28590592 | tf_op jit(solution)/shard_map/cond/branch_1_fun/while/body/eval_jaxpr/qhk,khd->qhd/dot_general | solution.py:39
  231.6 11.5 %fusion.85 = f32[512]{0:T(512)S(1)} fusion(f32[512,12288]{1,0:T(8,128)} %get-tuple-element.419, f32[512]{0:T(512)S(1)} %get-tuple-element.421, pred[12288]{0:T(1024)(128)(4,1)S(1)} %reduce.21), kind=kLoop, calls=%fused_computation.3.clone.1 | loop fusion | flops 25165312 | bytes 25182208 | tf_op jit(solution)/shard_map/cond/branch_1_fun/while/body/eval_jaxpr/reduce_sum | solution.py:38
  243.8 12.2 %fusion.84 = (f32[512]{0:T(512)S(1)}, f32[512,12288]{1,0:T(8,128)}) fusion(pred[12288]{0:T(1024)(128)(4,1)S(1)} %reduce.21, bf16[12288,1,128]{2,0,1:T(8,128)(2,1)} %get-tuple-element.487, bf16[6,512,1,128]{3,1,2,0:T(8,128)(2,1)S(1)} %get-tuple-element.486, s32[]{:T(128)} %get-tuple-element.471), kind=kOutput, calls=%fused_computation.4.clone.1 | convolution fusion | flops 1629486592 | bytes 28456964 | tf_op jit(solution)/shard_map/cond/branch_1_fun/while/body/eval_jaxpr/qhd,khd->qhk/dot_general | solution.py:31
  256.1 11.9 %fusion.86 = f32[6,512,1,128]{3,1,2,0:T(8,128)} fusion(f32[6,512,1,128]{3,1,2,0:T(8,128)} %get-tuple-element.474, s32[]{:T(128)} %get-tuple-element.471, bf16[12288,1,128]{2,0,1:T(8,128)(2,1)S(1)} %copy-done.6, f32[512,12288]{1,0:T(8,128)} %get-tuple-element.419, f32[512]{0:T(512)S(1)} %get-tuple-element.421, pred[12288]{0:T(1024)(128)(4,1)S(1)} %reduce.21, ...), kind=kOutput, calls=%fused_computation.14.clone.1 | convolution fusion | flops 1635844096 | bytes 28590592 | tf_op jit(solution)/shard_map/cond/branch_1_fun/while/body/eval_jaxpr/qhk,khd->qhd/dot_general | solution.py:39
  280.3 12.2 %fusion.84 = (f32[512]{0:T(512)S(1)}, f32[512,12288]{1,0:T(8,128)}) fusion(pred[12288]{0:T(1024)(128)(4,1)S(1)} %reduce.21, bf16[12288,1,128]{2,0,1:T(8,128)(2,1)} %get-tuple-element.487, bf16[6,512,1,128]{3,1,2,0:T(8,128)(2,1)S(1)} %get-tuple-element.486, s32[]{:T(128)} %get-tuple-element.471), kind=kOutput, calls=%fused_computation.4.clone.1 | convolution fusion | flops 1629486592 | bytes 28456964 | tf_op jit(solution)/shard_map/cond/branch_1_fun/while/body/eval_jaxpr/qhd,khd->qhk/dot_general | solution.py:31
  292.5 11.9 %fusion.86 = f32[6,512,1,128]{3,1,2,0:T(8,128)} fusion(f32[6,512,1,128]{3,1,2,0:T(8,128)} %get-tuple-element.474, s32[]{:T(128)} %get-tuple-element.471, bf16[12288,1,128]{2,0,1:T(8,128)(2,1)S(1)} %copy-done.6, f32[512,12288]{1,0:T(8,128)} %get-tuple-element.419, f32[512]{0:T(512)S(1)} %get-tuple-element.421, pred[12288]{0:T(1024)(128)(4,1)S(1)} %reduce.21, ...), kind=kOutput, calls=%fused_computation.14.clone.1 | convolution fusion | flops 1635844096 | bytes 28590592 | tf_op jit(solution)/shard_map/cond/branch_1_fun/while/body/eval_jaxpr/qhk,khd->qhd/dot_general | solution.py:39
  304.4 11.5 %fusion.85 = f32[512]{0:T(512)S(1)} fusion(f32[512,12288]{1,0:T(8,128)} %get-tuple-element.419, f32[512]{0:T(512)S(1)} %get-tuple-element.421, pred[12288]{0:T(1024)(128)(4,1)S(1)} %reduce.21), kind=kLoop, calls=%fused_computation.3.clone.1 | loop fusion | flops 25165312 | bytes 25182208 | tf_op jit(solution)/shard_map/cond/branch_1_fun/while/body/eval_jaxpr/reduce_sum | solution.py:38
  316.7 12.2 %fusion.84 = (f32[512]{0:T(512)S(1)}, f32[512,12288]{1,0:T(8,128)}) fusion(pred[12288]{0:T(1024)(128)(4,1)S(1)} %reduce.21, bf16[12288,1,128]{2,0,1:T(8,128)(2,1)} %get-tuple-element.487, bf16[6,512,1,128]{3,1,2,0:T(8,128)(2,1)S(1)} %get-tuple-element.486, s32[]{:T(128)} %get-tuple-element.471), kind=kOutput, calls=%fused_computation.4.clone.1 | convolution fusion | flops 1629486592 | bytes 28456964 | tf_op jit(solution)/shard_map/cond/branch_1_fun/while/body/eval_jaxpr/qhd,khd->qhk/dot_general | solution.py:31
  328.9 11.9 %fusion.86 = f32[6,512,1,128]{3,1,2,0:T(8,128)} fusion(f32[6,512,1,128]{3,1,2,0:T(8,128)} %get-tuple-element.474, s32[]{:T(128)} %get-tuple-element.471, bf16[12288,1,128]{2,0,1:T(8,128)(2,1)S(1)} %copy-done.6, f32[512,12288]{1,0:T(8,128)} %get-tuple-element.419, f32[512]{0:T(512)S(1)} %get-tuple-element.421, pred[12288]{0:T(1024)(128)(4,1)S(1)} %reduce.21, ...), kind=kOutput, calls=%fused_computation.14.clone.1 | convolution fusion | flops 1635844096 | bytes 28590592 | tf_op jit(solution)/shard_map/cond/branch_1_fun/while/body/eval_jaxpr/qhk,khd->qhd/dot_general | solution.py:39
  352.9 41.5 %conditional.3 = ((f32[3072,1]{0,1:T(1,128)}, f32[3072,1,128]{2,0,1:T(8,128)})) conditional(s32[]{:T(128)} %convert_element_type.43, (f32[3072,1]{0,1:T(1,128)}, f32[3072,1,128]{2,0,1:T(8,128)}) %tuple.30, (bf16[3072,1,128]{2,0,1:T(8,128)(2,1)S(1)}, f32[3072,1]{0,1:T(1,128)}, f32[3072,1]{0,1:T(1,128)}, f32[3072,1,128]{2,0,1:T(8,128)}, ...), branch_computations={%region_12.13_spmd, %region_13.18_spmd} | conditional | flops 816452608 | bytes 24337152 | solution.py:60
  353.0 38.2 %while.25 = (s32[]{:T(128)}, f32[6,512,1]{1,2,0:T(1,128)S(1)}, f32[6,512,1,128]{3,1,2,0:T(8,128)}, f32[6,512,1]{1,2,0:T(1,128)}, f32[6,512,1]{1,2,0:T(1,128)}, /...) while((s32[]{:T(128)}, f32[6,512,1]{1,2,0:T(1,128)S(1)}, ...), condition=%wide.region_17.17_spmd, body=%wide.region_14.16_spmd.sunk | while | flops 816449536 | bytes 21145216 | solution.py:54
  410.0 13.4 %all-to-all-done.3 = bf16[32,2,6144]{2,1,0:T(2,128)(2,1)S(1)} async-done(((bf16[32,2,6144]{2,1,0:T(2,128)(2,1)}), bf16[32,2,6144]{2,1,0:T(2,128)(2,1)S(1)}, u32[]{:S(2)}, u32[]{:S(2)}) %all-to-all-start.3) | async-done | bytes 786464 | tf_op jit(solution)/shard_map/all_to_all | solution.py:118
  (136 shorter events, 126.4 us)
Async XLA Ops:
  6.5 46.0 %copy-start.1 = (bf16[1,96,4096]{2,1,0:T(8,128)(2,1)S(1)}, bf16[1,96,4096]{2,1,0:T(8,128)(2,1)}, u32[]{:S(2)}) copy-start(bf16[1,96,4096]{2,1,0:T(8,128)(2,1)} %param.17) | copy-start | bytes 2359300
  6.5 88.5 %all-gather.5.cloned.1.call-start = ((), (), s32[]{:S(2)}) async-start(), calls=%async_computation.4 | async-start | bytes 3932160 | tf_op jit(solution)/shard_map/all_gather | solution.py:97
  8.2 51.6 %copy-start.5 = (s32[4]{0:T(128)S(1)}, s32[4]{0:T(128)}, u32[]{:S(2)}) copy-start(s32[4]{0:T(128)} %param.24) | copy-start | bytes 52
  8.2 54.4 %copy-start.4 = (s32[4,8]{1,0:T(4,128)S(1)}, s32[4,8]{1,0:T(4,128)}, u32[]{:S(2)}) copy-start(s32[4,8]{1,0:T(4,128)} %param.25) | copy-start | bytes 388
  8.2 56.0 %copy-start.2 = (bf16[768,128]{1,0:T(8,128)(2,1)S(1)}, bf16[768,128]{1,0:T(8,128)(2,1)}, u32[]{:S(2)}) copy-start(bf16[768,128]{1,0:T(8,128)(2,1)} %param.20) | copy-start | bytes 589828
  33.4 49.1 %copy-start.3 = (bf16[768,128]{1,0:T(8,128)(2,1)S(1)}, bf16[768,128]{1,0:T(8,128)(2,1)}, u32[]{:S(2)}) copy-start(bf16[768,128]{1,0:T(8,128)(2,1)} %param.21) | copy-start | bytes 589828
  33.4 100.4 %all-gather.7.cloned.1.call-start = ((), (), s32[]{:S(2)}) async-start(), calls=%async_computation.5 | async-start | bytes 3932160 | tf_op jit(solution)/shard_map/all_gather | solution.py:98
  53.9 41.2 %all-to-all-start = ((bf16[96,32,128]{2,0,1:T(8,128)(2,1)}), bf16[96,32,128]{2,0,1:T(8,128)(2,1)S(1)}, u32[]{:S(2)}, u32[]{:S(2)}) async-start(bf16[96,32,128]{2,0,1:T(8,128)(2,1)} %copy.42), calls=%async_computation | async-start | bytes 1572864 | tf_op jit(solution)/shard_map/all_to_all | solution.py:83
  134.6 12.3 %copy-start.6 = (bf16[12288,1,128]{2,0,1:T(8,128)(2,1)S(1)}, bf16[12288,1,128]{2,0,1:T(8,128)(2,1)}, u32[]{:S(2)}) copy-start(bf16[12288,1,128]{2,0,1:T(8,128)(2,1)} %get-tuple-element.488) | copy-start | bytes 9437188 | tf_op jit(solution)/shard_map/cond/branch_1_fun/while
  171.0 12.3 %copy-start.6 = (bf16[12288,1,128]{2,0,1:T(8,128)(2,1)S(1)}, bf16[12288,1,128]{2,0,1:T(8,128)(2,1)}, u32[]{:S(2)}) copy-start(bf16[12288,1,128]{2,0,1:T(8,128)(2,1)} %get-tuple-element.488) | copy-start | bytes 9437188 | tf_op jit(solution)/shard_map/cond/branch_1_fun/while
  207.4 12.3 %copy-start.6 = (bf16[12288,1,128]{2,0,1:T(8,128)(2,1)S(1)}, bf16[12288,1,128]{2,0,1:T(8,128)(2,1)}, u32[]{:S(2)}) copy-start(bf16[12288,1,128]{2,0,1:T(8,128)(2,1)} %get-tuple-element.488) | copy-start | bytes 9437188 | tf_op jit(solution)/shard_map/cond/branch_1_fun/while
  243.8 12.3 %copy-start.6 = (bf16[12288,1,128]{2,0,1:T(8,128)(2,1)S(1)}, bf16[12288,1,128]{2,0,1:T(8,128)(2,1)}, u32[]{:S(2)}) copy-start(bf16[12288,1,128]{2,0,1:T(8,128)(2,1)} %get-tuple-element.488) | copy-start | bytes 9437188 | tf_op jit(solution)/shard_map/cond/branch_1_fun/while
  280.3 12.3 %copy-start.6 = (bf16[12288,1,128]{2,0,1:T(8,128)(2,1)S(1)}, bf16[12288,1,128]{2,0,1:T(8,128)(2,1)}, u32[]{:S(2)}) copy-start(bf16[12288,1,128]{2,0,1:T(8,128)(2,1)} %get-tuple-element.488) | copy-start | bytes 9437188 | tf_op jit(solution)/shard_map/cond/branch_1_fun/while
  316.7 12.3 %copy-start.6 = (bf16[12288,1,128]{2,0,1:T(8,128)(2,1)S(1)}, bf16[12288,1,128]{2,0,1:T(8,128)(2,1)}, u32[]{:S(2)}) copy-start(bf16[12288,1,128]{2,0,1:T(8,128)(2,1)} %get-tuple-element.488) | copy-start | bytes 9437188 | tf_op jit(solution)/shard_map/cond/branch_1_fun/while
  394.5 13.9 %copy-start.7 = (s32[4]{0:T(128)S(1)}, s32[4]{0:T(128)}, u32[]{:S(2)}) copy-start(s32[4]{0:T(128)} %param.23) | copy-start | bytes 52
  394.5 15.3 %copy-start = (f32[64,4096]{1,0:T(8,128)S(1)}, f32[64,4096]{1,0:T(8,128)}, u32[]{:S(2)}) copy-start(f32[64,4096]{1,0:T(8,128)} %param.22) | copy-start | bytes 3145732
  399.3 24.1 %all-to-all-start.3 = ((bf16[32,2,6144]{2,1,0:T(2,128)(2,1)}), bf16[32,2,6144]{2,1,0:T(2,128)(2,1)S(1)}, u32[]{:S(2)}, u32[]{:S(2)}) async-start(bf16[32,2,6144]{2,1,0:T(2,128)(2,1)} %reshape.401), calls=%async_computation.3 | async-start | bytes 1572864 | tf_op jit(solution)/shard_map/all_to_all | solution.py:118
Sparse Core Ops, SparseCore 0:
  33.5 60.0 all-gather.4
  95.3 38.4 all-gather.6
where the time goes:
time: 436 us; the launch traced here: 435 us
  matrix products  168 us (39%)
  other arithmetic  95.2 us (22%)
  blocking collectives  73.2 us (17%)
  waiting for transfers between devices  52.2 us (12%)
  local copies, waits for them, and re-layouts  15.5 us (4%)
  starting transfers between devices  15.1 us (3%)
  between operations  15 us (3%)
    dot_general x12, matrix products, one_block(): jnp.einsum('qhk,khd->qhd', weights.astype(jnp.bfloat16), piece_values, pr...  88 us
    dot_general x12, matrix products, one_block(): jnp.einsum('qhd,khd->qhk', query_block, piece_keys, preferred_element_typ...  80.5 us
    reduce_sum x12, other arithmetic, one_block(): total_block = total_block * rescale + jnp.sum(weights, axis=2)  75 us
    all_gather x1, waiting for transfers between devices, on_device(): piece_values = lax.all_gather(head_values, 'span', axis=0, tiled=True)  38.7 us
    all_to_all x1, blocking collectives, on_device(): lax.all_to_all(row_keys, 'cp', split_axis=1, concat_axis=0, tiled=True)  25.1 us
    all_gather x1, blocking collectives, on_device(): piece_keys = lax.all_gather(local_cache_keys, 'span', axis=0, tiled=True)  18.1 us
    all_to_all x1, blocking collectives, on_device(): lax.all_to_all(row_values, 'cp', split_axis=1, concat_axis=0, tiled=True)  17.4 us
    all_to_all x1, waiting for transfers between devices, on_device(): lax.all_to_all(attention[0], 'cp', split_axis=0, concat_axis=1, tiled=True)  13.4 us
  transfers between devices with their start and end apart: 4, of which 2 were waited for; matrix products, arithmetic and copies ran while one was open for 2% of the time, Pallas kernels for 0%

commit v1 on v0

v1 whole, which is shorter than its diff:
```python
import math

import jax
import jax.numpy as jnp
from jax import lax
from jax.experimental import pallas as pl
from jax.experimental.pallas import tpu as pltpu
from jax.sharding import PartitionSpec as P

H = 32
HD = 128
NBLK = 8
SPANS = 4
ROWS = 768
HALF = 1536
SPAN_TOK = 3072
BLK = SPAN_TOK // NBLK
SUB = 256
SCALE = math.log2(math.e) / math.sqrt(HD)
LOW = -1e30
NT = (((1,), (1,)), ((), ()))
CORE_SWAP = [(0, 1), (1, 0), (2, 3), (3, 2)]
CHIP_SWAP = [(0, 2), (2, 0), (1, 3), (3, 1)]


def lane_sums(p):
    total = p[:, :HD]
    for t in range(1, p.shape[1] // HD):
        total = total + p[:, t * HD : (t + 1) * HD]
    return total


def attention_kernel(
    order, by_order, seen, q_ref, ka, va, kb, vb, ck, cv, o_ref, q2_s, m_s, l_s, acc_s
):
    c = pl.program_id(0)
    x = q_ref[...].astype(jnp.float32) * SCALE
    hi = x.astype(jnp.bfloat16)
    lo = (x - hi.astype(jnp.float32)).astype(jnp.bfloat16)
    q2_s[...] = jnp.concatenate([hi, lo], axis=1)
    count = order[c] + 1
    parts = [slice(j * SUB, (j + 1) * SUB) for j in range(ROWS // SUB)]

    def scores(rows, k):
        k2 = jnp.concatenate([k, k], axis=1)
        return lax.dot_general(q2_s[rows, :], k2, NT, preferred_element_type=jnp.float32)

    def half(ref, span):
        return ref[span].reshape(HALF, HD)

    def both(ref_a, ref_b, span):
        return jnp.concatenate([half(ref_a, span), half(ref_b, span)], axis=0)

    first = half(ka, c)[:SUB]
    for rows in parts:
        top = jnp.max(scores(rows, first), axis=1, keepdims=True)
        m_s[rows, :] = jnp.broadcast_to(top, (SUB, HD))
    l_s[...] = jnp.zeros_like(l_s)
    acc_s[...] = jnp.zeros_like(acc_s)

    def add(rows, p, v):
        l_s[rows, :] += lane_sums(p)
        acc_s[rows, :] += jnp.dot(p.astype(jnp.bfloat16), v, preferred_element_type=jnp.float32)

    def span_step(i, carry):
        span = by_order[i]
        k = both(ka, kb, span)
        v = both(va, vb, span)
        for rows in parts:
            shift = jnp.concatenate([m_s[rows, :]] * (SPAN_TOK // HD), axis=1)
            add(rows, jnp.exp2(scores(rows, k) - shift), v)
        return carry

    lax.fori_loop(0, count, span_step, 0)
    any_seen = seen[c, 0]
    for b in range(1, NBLK):
        any_seen = any_seen + seen[c, b]

    @pl.when(any_seen > 0)
    def _():
        k = ck[...]
        v = cv[...]
        for rows in parts:
            m = m_s[rows, :]
            shift = []
            for b in range(NBLK):
                shift += [jnp.where(seen[c, b] > 0, m, -LOW)] * (BLK // HD)
            add(rows, jnp.exp2(scores(rows, k) - jnp.concatenate(shift, axis=1)), v)

    fits = jnp.sum(l_s[...], axis=1, keepdims=True) < 2.0**100
    bad = jnp.max(jnp.where(fits, 0.0, 1.0))

    @pl.when(bad > 0.0)
    def _():
        m_s[...] = jnp.full_like(m_s, LOW)
        l_s[...] = jnp.zeros_like(l_s)
        acc_s[...] = jnp.zeros_like(acc_s)

        def careful(k, v):
            for rows in parts:
                s = scores(rows, k)
                m = m_s[rows, :]
                top = jnp.maximum(m, jnp.max(s, axis=1, keepdims=True))
                rescale = jnp.exp2(m - top)
                m_s[rows, :] = top
                l_s[rows, :] *= rescale
                acc_s[rows, :] *= rescale
                add(rows, jnp.exp2(s - jnp.concatenate([top] * (k.shape[0] // HD), axis=1)), v)

        def careful_span(i, carry):
            span = by_order[i]
            careful(half(ka, span), half(va, span))
            careful(half(kb, span), half(vb, span))
            return carry

        lax.fori_loop(0, count, careful_span, 0)

        def careful_block(b, carry):
            @pl.when(seen[c, b] > 0)
            def _():
                rows = pl.ds(pl.multiple_of(b * BLK, BLK), BLK)
                careful(ck[rows, :], cv[rows, :])

            return carry

        lax.fori_loop(0, NBLK, careful_block, 0)

    total = jnp.sum(l_s[...], axis=1, keepdims=True)
    o_ref[...] = (acc_s[...] / total).astype(o_ref.dtype)


def attention(order, by_order, seen, q, mine, other, ck, cv):
    whole = lambda part: pl.BlockSpec((SPANS, H, 1, 48, HD), lambda c, *_: (0, 0, part, 0, 0))
    cached = pl.BlockSpec((SPAN_TOK, HD), lambda c, *_: (0, 0))
    rows = pl.BlockSpec((ROWS, HD), lambda c, *_: (c, 0))
    mine = mine.reshape(SPANS, H, 2, 48, HD)
    other = other.reshape(SPANS, H, 2, 48, HD)
    return pl.pallas_call(
        attention_kernel,
        grid_spec=pltpu.PrefetchScalarGridSpec(
            num_scalar_prefetch=3,
            grid=(SPANS,),
            in_specs=[rows, whole(0), whole(1), whole(0), whole(1), cached, cached],
            out_specs=rows,
            scratch_shapes=[
                pltpu.VMEM((ROWS, 2 * HD), jnp.bfloat16),
                pltpu.VMEM((ROWS, HD), jnp.float32),
                pltpu.VMEM((ROWS, HD), jnp.float32),
                pltpu.VMEM((ROWS, HD), jnp.float32),
            ],
        ),
        out_shape=jax.ShapeDtypeStruct((SPANS * ROWS, HD), jnp.bfloat16),
        compiler_params=pltpu.CompilerParams(vmem_limit_bytes=48 * 2**20),
        cost_estimate=pl.CostEstimate(
            flops=16_000_000_000, bytes_accessed=12_000_000, transcendentals=30_000_000
        ),
        name="attention",
    )(order, by_order, seen, q, mine, mine, other, other, ck, cv)


def on_device(
    queries, keys, values, cache_keys, cache_values, gate_table, noise_steps, span_order, block_mask
):
    everyone = ("span", "cp")
    group = lax.axis_index("span")
    cache = jnp.concatenate([cache_keys, cache_values], axis=0)
    cache = jnp.stack([cache, lax.ppermute(cache, "span", CHIP_SWAP)])
    cache = jnp.concatenate([cache, lax.ppermute(cache, "span", CORE_SWAP)])
    ck = cache[:, :768].reshape(SPAN_TOK, HD)
    cv = cache[:, 768:].reshape(SPAN_TOK, HD)
    holders = jnp.stack([group, group ^ 2, group ^ 1, group ^ 3])
    slots = (holders[:, None] * 2 + jnp.arange(2)[None, :]).reshape(NBLK)
    seen = jnp.take(block_mask, slots, axis=1)
    by_order = jnp.sum(
        jnp.where(span_order[None, :] == jnp.arange(SPANS)[:, None], jnp.arange(SPANS)[None, :], 0),
        axis=1,
    ).astype(jnp.int32)

    q = queries.reshape(SPANS, 24, H, HD).transpose(0, 2, 1, 3).reshape(128, 24, HD)
    k = keys.reshape(2, 48, H, HD).transpose(0, 2, 1, 3)
    v = values.reshape(2, 48, H, HD).transpose(0, 2, 1, 3)
    kv = jnp.concatenate([k, v], axis=2)
    kv = jnp.concatenate([kv, kv], axis=0).reshape(128, 96, HD)
    q = lax.all_to_all(q, everyone, 0, 0, tiled=True)
    kv = lax.all_to_all(kv, everyone, 0, 0, tiled=True)
    other = lax.ppermute(kv, "span", CORE_SWAP)
    out = attention(
        span_order, by_order, seen, q.reshape(SPANS * ROWS, HD), kv, other, ck, cv
    )
    out = lax.all_to_all(out.reshape(128, 24, HD), everyone, 0, 0, tiled=True)
    out = out.reshape(SPANS, H, 24, HD).transpose(0, 2, 1, 3).reshape(96, H * HD)
    step = lax.dynamic_index_in_dim(noise_steps, group, 0, keepdims=False)
    gate_row = lax.dynamic_index_in_dim(gate_table, step, 0, keepdims=True)
    return (out.astype(jnp.float32) * gate_row).astype(jnp.bfloat16)[None]


def solution(mesh):
    placed = (
        P("span", "cp", None),
        P("span", "cp", None),
        P("span", "cp", None),
        P("span", "cp"),
        P("span", "cp"),
        P(),
        P(),
        P(),
        P(),
    )
    return jax.shard_map(
        on_device, mesh=mesh, in_specs=placed, out_specs=P("span", "cp", None), check_vma=False
    )
```

time: 436 us -> 212 us (0.49)
  matrix products: 168 us -> 0 us
  Pallas kernels: 0 us -> 103 us
  other arithmetic: 95.2 us -> 3.01 us
  waiting for transfers between devices: 52.2 us -> 25.9 us
  blocking collectives: 73.2 us -> 53.2 us
  between operations: 15 us -> 2.12 us
  local copies, waits for them, and re-layouts: 15.5 us -> 9.18 us
    dot_general x24 -> x0, matrix products: 168 us -> none  [the longest x12 88 us: one_block(): jnp.einsum('qhk,khd->qhd', weights.astype(jnp.bfloat16), piece_values, pr...]
    pallas_call x0 -> x1, Pallas kernels: none -> 103 us  [attention(): pl.pallas_call(attention_kernel, grid_spec=pltpu.PrefetchScalarGridSpec(n...]
    reduce_sum x18 -> x1, other arithmetic: 76.9 us -> 0.12 us  [on_device(): jnp.sum(jnp.where(span_order[None, :] == jnp.arange(SPANS)[:, None], jnp....]
    all_gather x2 -> x0, waiting for transfers between devices: 38.7 us -> none  [the longest x1 38.7 us: on_device(): piece_values = lax.all_gather(head_values, 'span', axis=0, tiled=True)]
    all_gather x2 -> x0, blocking collectives: 30.7 us -> none  [the longest x1 18.1 us: on_device(): piece_keys = lax.all_gather(local_cache_keys, 'span', axis=0, tiled=True)]
    ppermute x0 -> x3, waiting for transfers between devices: none -> 11.8 us  [the longest x1 10.6 us: on_device(): cache = jnp.stack([cache, lax.ppermute(cache, 'span', CHIP_SWAP)])]
    all_to_all x2 -> x1, blocking collectives: 42.5 us -> 53.2 us  [on_device(): kv = lax.all_to_all(kv, everyone, 0, 0, tiled=True)]
    dynamic_update_slice x12 -> x0, other arithmetic: 7.87 us -> none  [update(): mapped = lax.map(one_block, shaped)]
  transfers between devices with their start and end apart: 4 -> 5, of which waited for: 2 -> 3; matrix products, arithmetic and copies ran while one was open for 2% -> 2% of each run, Pallas kernels for 0% -> 0%
where the time goes in v1:
time: 212 us; the launch traced here: 209 us
  Pallas kernels  103 us (49%)
  blocking collectives  53.2 us (25%)
  waiting for transfers between devices  25.9 us (12%)
  starting transfers between devices  12.3 us (6%)
  local copies, waits for them, and re-layouts  9.18 us (4%)
  other arithmetic  3.01 us (1%)
  between operations  2.12 us (1%)
    pallas_call x1, Pallas kernels, attention(): pl.pallas_call(attention_kernel, grid_spec=pltpu.PrefetchScalarGridSpec(n...  103 us
    all_to_all x1, blocking collectives, on_device(): kv = lax.all_to_all(kv, everyone, 0, 0, tiled=True)  53.2 us
    all_to_all x1, waiting for transfers between devices, on_device(): out = lax.all_to_all(out.reshape(128, 24, HD), everyone, 0, 0, tiled=True)  14.1 us
    ppermute x1, waiting for transfers between devices, on_device(): cache = jnp.stack([cache, lax.ppermute(cache, 'span', CHIP_SWAP)])  10.6 us
  transfers between devices with their start and end apart: 5, of which 3 were waited for; matrix products, arithmetic and copies ran while one was open for 2% of the time, Pallas kernels for 0%

profile of v1, /device:TPU:1, one launch (start us, length us, event | category | flops | bytes accessed | tf_op | source)
XLA Modules:
  0.0 208.9 jit_solution(4422373187100255512)
XLA Ops:
  0.0 1.4 copy.26
  1.5 0.2 copy.27
  1.6 0.3 bitcast_bitcast_fusion
  1.9 0.4 maximum_maximum_fusion
  2.3 1.2 copy.23
  3.6 53.2 %all_to_all.15 = bf16[128,96,128]{2,1,0:T(8,128)(2,1)} all-to-all(bf16[128,96,128]{2,1,0:T(8,128)(2,1)S(1)} %bitcast.53), channel_id=1, replica_groups=mesh['span'=4,'cp'=32] {'span','cp'}, dimensions={0} | all-to-all | bytes 6291456 | tf_op jit(solution)/shard_map/all_to_all | solution.py:185
  56.7 1.2 collective-permute-start
  58.1 0.2 copy.25
  58.3 1.2 copy.22
  59.5 4.1 %all-to-all-start = ((bf16[128,24,128]{2,1,0:T(8,128)(2,1)}), bf16[128,24,128]{2,1,0:T(8,128)(2,1)S(1)}, u32[]{:S(2)}, u32[]{:S(2)}) async-start(bf16[128,24,128]{2,1,0:T(8,128)(2,1)} %bitcast.7), calls=%async_computation | async-start | bytes 1572864 | tf_op jit(solution)/shard_map/all_to_all | solution.py:184
  64.0 10.6 %collective-permute-done.1 = bf16[1536,128]{1,0:T(8,128)(2,1)S(1)} collective-permute-done((bf16[1536,128]{1,0:T(8,128)(2,1)S(1)}, bf16[1536,128]{1,0:T(8,128)(2,1)S(1)}, u32[]{:S(2)}, u32[]{:S(2)}) %collective-permute-start.1) | collective-permute-done | bytes 393248 | tf_op jit(solution)/shard_map/ppermute | solution.py:167
  74.7 3.0 %collective-permute-start.2 = (bf16[2,1536,128]{2,1,0:T(8,128)(2,1)S(1)}, bf16[2,1536,128]{2,1,0:T(8,128)(2,1)}, u32[]{:S(2)}, u32[]{:S(2)}) collective-permute-start(bf16[2,1536,128]{2,1,0:T(8,128)(2,1)S(1)} %pad_maximum_fusion.1), channel_id=1, source_target_pairs={{0,32},{32,0},{64,96},{96,64},{1,33},{33,1},{65,97},{97,65},{2,34}... | collective-permute-start | bytes 2359304 | tf_op jit(solution)/shard_map/ppermute | solution.py:168
  77.7 0.6 gather_fusion
  78.3 0.1 select_reduce_fusion.by_order
  78.4 1.3 collective-permute-done.2
  79.7 1.3 pad_maximum_fusion
  81.0 0.1 fusion.1
  81.1 103.2 %attention.1 = bf16[3072,128]{1,0:T(8,128)(2,1)} custom-call(s32[4]{0:T(128)S(1)} %copy-done.1, s32[4]{0:T(128)S(1)} %select_reduce_fusion.by_order, s32[4,8]{1,0:T(4,128)S(1)} %select_bitcast_fusion.seen, bf16[3072,128]{1,0:T(8,128)(2,1)S(1)} %bitcast.50, bf16[4,32,2,48,128]{4,3,2,1,0:T(8,128)(2,1)} %bitcast.12.ka.va, ...), custom_call_target="tpu_custom_call" | custom-call | flops 16000000000 | bytes 12000000 | tf_op jit(solution)/shard_map/attention/pallas_call | solution.py:138
  184.4 3.9 %all-to-all-start.2 = ((bf16[128,24,128]{2,1,0:T(8,128)(2,1)}), bf16[128,24,128]{2,1,0:T(8,128)(2,1)S(1)}, u32[]{:S(2)}, u32[]{:S(2)}) async-start(bf16[128,24,128]{2,1,0:T(8,128)(2,1)} %bitcast.18), calls=%async_computation.2 | async-start | bytes 1572864 | tf_op jit(solution)/shard_map/all_to_all | solution.py:190
  188.3 0.6 dynamic_slice.8
  190.9 14.1 %all-to-all-done.2 = bf16[128,24,128]{2,1,0:T(8,128)(2,1)S(1)} async-done(((bf16[128,24,128]{2,1,0:T(8,128)(2,1)}), bf16[128,24,128]{2,1,0:T(8,128)(2,1)S(1)}, u32[]{:S(2)}, u32[]{:S(2)}) %all-to-all-start.2) | async-done | bytes 786464 | tf_op jit(solution)/shard_map/all_to_all | solution.py:190
  204.9 1.4 copy.29
  206.3 1.6 reshape.164
  207.9 1.0 multiply_convert_fusion
  (34 shorter events, 0.9 us)
Async XLA Ops:
  0.0 190.8 %copy-start = (f32[64,4096]{1,0:T(8,128)S(1)}, f32[64,4096]{1,0:T(8,128)}, u32[]{:S(2)}) copy-start(f32[64,4096]{1,0:T(8,128)} %param.14) | copy-start | bytes 3145732
  0.0 1.5 copy-start.2
  3.5 54.4 %copy-start.4 = (bf16[768,128]{1,0:T(8,128)(2,1)S(1)}, bf16[768,128]{1,0:T(8,128)(2,1)}, u32[]{:S(2)}) copy-start(bf16[768,128]{1,0:T(8,128)(2,1)} %param.12) | copy-start | bytes 589828
  3.5 54.4 %copy-start.5 = (bf16[768,128]{1,0:T(8,128)(2,1)S(1)}, bf16[768,128]{1,0:T(8,128)(2,1)}, u32[]{:S(2)}) copy-start(bf16[768,128]{1,0:T(8,128)(2,1)} %param.13) | copy-start | bytes 589828
  3.6 54.5 %copy-start.3 = (bf16[1,96,4096]{2,1,0:T(8,128)(2,1)S(1)}, bf16[1,96,4096]{2,1,0:T(8,128)(2,1)}, u32[]{:S(2)}) copy-start(bf16[1,96,4096]{2,1,0:T(8,128)(2,1)} %param.9) | copy-start | bytes 2359300
  56.7 24.4 %collective-permute-start = (bf16[128,96,128]{2,1,0:T(8,128)(2,1)}, bf16[128,96,128]{2,1,0:T(8,128)(2,1)}, u32[]{:S(2)}, u32[]{:S(2)}) collective-permute-start(bf16[128,96,128]{2,1,0:T(8,128)(2,1)} %all_to_all.15), channel_id=1, source_target_pairs={{0,32},{32,0},{64,96},{96,64},{1,33},{33,1},{65,97},{97,65},{2,34}... | collective-permute-start | bytes 9437192 | tf_op jit(solution)/shard_map/ppermute | solution.py:186
  58.0 16.6 %collective-permute-start.1 = (bf16[1536,128]{1,0:T(8,128)(2,1)S(1)}, bf16[1536,128]{1,0:T(8,128)(2,1)S(1)}, u32[]{:S(2)}, u32[]{:S(2)}) collective-permute-start(bf16[1536,128]{1,0:T(8,128)(2,1)S(1)} %constant_dynamic-update-slice_fusion), channel_id=1, source_target_pairs={{0,64},{64,0},{32,96},{96,32},{1,65},{65,1},{33,97},{97,33},{2,66}... | collective-permute-start | bytes 1179656 | tf_op jit(solution)/shard_map/ppermute | solution.py:167
  58.3 5.6 %copy-start.6 = (s32[4,8]{1,0:T(4,128)S(1)}, s32[4,8]{1,0:T(4,128)}, u32[]{:S(2)}) copy-start(s32[4,8]{1,0:T(4,128)} %param.17) | copy-start | bytes 388
  59.5 18.8 %copy-start.1 = (s32[4]{0:T(128)S(1)}, s32[4]{0:T(128)}, u32[]{:S(2)}) copy-start(s32[4]{0:T(128)} %order.1) | copy-start | bytes 52
  59.5 21.6 %all-to-all-start = ((bf16[128,24,128]{2,1,0:T(8,128)(2,1)}), bf16[128,24,128]{2,1,0:T(8,128)(2,1)S(1)}, u32[]{:S(2)}, u32[]{:S(2)}) async-start(bf16[128,24,128]{2,1,0:T(8,128)(2,1)} %bitcast.7), calls=%async_computation | async-start | bytes 1572864 | tf_op jit(solution)/shard_map/all_to_all | solution.py:184
  74.7 5.0 %collective-permute-start.2 = (bf16[2,1536,128]{2,1,0:T(8,128)(2,1)S(1)}, bf16[2,1536,128]{2,1,0:T(8,128)(2,1)}, u32[]{:S(2)}, u32[]{:S(2)}) collective-permute-start(bf16[2,1536,128]{2,1,0:T(8,128)(2,1)S(1)} %pad_maximum_fusion.1), channel_id=1, source_target_pairs={{0,32},{32,0},{64,96},{96,64},{1,33},{33,1},{65,97},{97,65},{2,34}... | collective-permute-start | bytes 2359304 | tf_op jit(solution)/shard_map/ppermute | solution.py:168
  184.4 3.9 %copy-start.7 = (s32[4]{0:T(128)S(1)}, s32[4]{0:T(128)}, u32[]{:S(2)}) copy-start(s32[4]{0:T(128)} %param.15) | copy-start | bytes 52
  184.4 20.6 %all-to-all-start.2 = ((bf16[128,24,128]{2,1,0:T(8,128)(2,1)}), bf16[128,24,128]{2,1,0:T(8,128)(2,1)S(1)}, u32[]{:S(2)}, u32[]{:S(2)}) async-start(bf16[128,24,128]{2,1,0:T(8,128)(2,1)} %bitcast.18), calls=%async_computation.2 | async-start | bytes 1572864 | tf_op jit(solution)/shard_map/all_to_all | solution.py:190

commit v2 on v0

v2 whole, which is shorter than its diff:
```python
import math

import jax
import jax.numpy as jnp
from jax import lax
from jax.experimental import pallas as pl
from jax.experimental.pallas import tpu as pltpu
from jax.sharding import PartitionSpec as P

H = 32
HD = 128
NBLK = 8
SPANS = 4
ROWS = 768
SPAN_TOK = 3072
BLK = SPAN_TOK // NBLK
PART = 24
SUB = 256
SCALE = math.log2(math.e) / math.sqrt(HD)
LOW = -1e30
NT = (((1,), (1,)), ((), ()))
CORE_SWAP = [(0, 1), (1, 0), (2, 3), (3, 2)]
CHIP_SWAP = [(0, 2), (2, 0), (1, 3), (3, 1)]
EVERYONE = ("span", "cp")
MEMORY = 60 * 2**20


def pack_kernel(k_ref, v_ref, q_ref, o_ref):
    heads = o_ref.shape[1]
    for h in range(heads):
        cols = slice(h * HD, (h + 1) * HD)
        k, v, q = (ref[0, :, cols].astype(jnp.float32) for ref in (k_ref, v_ref, q_ref))
        for s in range(SPANS):
            rows = slice(s * PART, (s + 1) * PART)
            together = jnp.concatenate([k[rows], v[rows], q[rows]], axis=0)
            o_ref[s, h] = together.astype(o_ref.dtype)


def pack(k, v, q):
    step = 16
    return pl.pallas_call(
        pack_kernel,
        grid=(H // step,),
        in_specs=[pl.BlockSpec((1, SPANS * PART, step * HD), lambda j: (0, 0, j))] * 3,
        out_specs=pl.BlockSpec((SPANS, step, 3 * PART, HD), lambda j: (0, j, 0, 0)),
        out_shape=jax.ShapeDtypeStruct((SPANS, H, 3 * PART, HD), jnp.bfloat16),
        compiler_params=pltpu.CompilerParams(vmem_limit_bytes=MEMORY),
        name="pack",
    )(k, v, q)


def gate_kernel(group, steps, x_ref, gate_ref, o_ref):
    heads = x_ref.shape[1]
    row = gate_ref[pl.ds(lax.rem(steps[group[0]], 8), 1), :]
    for h in range(heads):
        cols = slice(h * HD, (h + 1) * HD)
        x = [x_ref[s, h].astype(jnp.float32) for s in range(SPANS)]
        o_ref[0, :, cols] = (jnp.concatenate(x, axis=0) * row[:, cols]).astype(o_ref.dtype)


def apply_gate(group, steps, x, gate_table):
    step = 16
    return pl.pallas_call(
        gate_kernel,
        grid_spec=pltpu.PrefetchScalarGridSpec(
            num_scalar_prefetch=2,
            grid=(H // step,),
            in_specs=[
                pl.BlockSpec((SPANS, step, PART, HD), lambda j, *_: (0, j, 0, 0)),
                pl.BlockSpec(
                    (8, step * HD),
                    lambda j, group, steps: (lax.div(steps[group[0]], 8), j),
                ),
            ],
            out_specs=pl.BlockSpec((1, SPANS * PART, step * HD), lambda j, *_: (0, 0, j)),
        ),
        out_shape=jax.ShapeDtypeStruct((1, SPANS * PART, H * HD), jnp.bfloat16),
        compiler_params=pltpu.CompilerParams(vmem_limit_bytes=MEMORY),
        name="gate",
    )(group, steps, x, gate_table)


def lane_sums(p):
    total = p[:, :HD]
    for t in range(1, p.shape[1] // HD):
        total = total + p[:, t * HD : (t + 1) * HD]
    return total


def wide(column, width):
    return jnp.concatenate([column] * (width // HD), axis=1)


class Block:
    def __init__(self, q2, l, acc):
        self.q2, self.l, self.acc = q2, l, acc
        self.parts = [slice(j, j + SUB) for j in range(0, ROWS, SUB)]

    def load(self, q):
        x = q.astype(jnp.float32) * SCALE
        hi = x.astype(jnp.bfloat16)
        lo = (x - hi.astype(jnp.float32)).astype(jnp.bfloat16)
        self.q2[...] = jnp.concatenate([hi, lo], axis=1)

    def scores(self, rows, k):
        k2 = jnp.concatenate([k, k], axis=1)
        return lax.dot_general(self.q2[rows, :], k2, NT, preferred_element_type=jnp.float32)

    def clear(self):
        self.l[...] = jnp.zeros(self.l.shape, jnp.float32)
        self.acc[...] = jnp.zeros(self.acc.shape, jnp.float32)

    def add(self, rows, p, v):
        self.l[rows, :] += lane_sums(p)
        self.acc[rows, :] += jnp.dot(
            p.astype(jnp.bfloat16), v, preferred_element_type=jnp.float32
        )

    def fast(self, k, v, seen=None):
        for rows in self.parts:
            s = self.scores(rows, k)
            if seen is not None:
                s = jnp.concatenate(
                    [
                        s[:, b * BLK : (b + 1) * BLK] + jnp.where(one > 0, 0.0, LOW)
                        for b, one in enumerate(seen)
                    ],
                    axis=1,
                )
            self.add(rows, jnp.exp2(s), v)

    def careful(self, m, k, v):
        for rows in self.parts:
            s = self.scores(rows, k)
            old = m[rows, :]
            top = jnp.maximum(old, jnp.max(s, axis=1, keepdims=True))
            rescale = jnp.exp2(old - top)
            m[rows, :] = top
            self.l[rows, :] *= rescale
            self.acc[rows, :] *= rescale
            self.add(rows, jnp.exp2(s - wide(top, k.shape[0])), v)

    def finish(self, o_ref):
        total = jnp.sum(self.l[...], axis=1, keepdims=True)
        o_ref[...] = (self.acc[...] / total).astype(o_ref.dtype)
        fits = (total < 2.0**100) & (total > 2.0**-100)
        return jnp.max(jnp.where(fits, 0.0, 1.0)) > 0.0


def span_at(order, position):
    found = jnp.int32(0)
    for c in range(1, SPANS):
        found = jnp.where(order[c] == position, c, found)
    return found


class Loads:
    def __init__(self, groups, sems):
        self.groups, self.sems = groups, sems

    def copies(self, g):
        return [
            pltpu.make_async_copy(src, dst, self.sems.at[g, n])
            for n, (src, dst) in enumerate(self.groups(g))
        ]

    def start(self, g):
        for copy in self.copies(g):
            copy.start()

    def wait(self, g):
        for copy in self.copies(g):
            copy.wait()


def span_loads(ka, va, kb, vb, k_s, v_s, sems):
    low, high = pl.ds(0, ROWS), pl.ds(ROWS, ROWS)

    def group(span):
        return [
            (ka.at[span], k_s.at[span, low]),
            (kb.at[span], k_s.at[span, high]),
            (va.at[span], v_s.at[span, low]),
            (vb.at[span], v_s.at[span, high]),
        ]

    return Loads(group, sems)


def blocks_seen(group, mask, c):
    holders = [lax.bitwise_xor(group[0], jnp.int32(x)) for x in (0, 2, 1, 3)]
    return [mask[c, holder * 2 + b] for holder in holders for b in range(2)]


def over_spans(order, c, loads, block, k_s, v_s):
    count = order[c] + 1

    def arrive(i):
        @pl.when(c == 0)
        def _():
            loads.wait(span_at(order, i))

    def two(i, carry):
        arrive(2 * i)
        arrive(2 * i + 1)
        one, other = span_at(order, 2 * i), span_at(order, 2 * i + 1)
        block.fast(
            jnp.concatenate([k_s[one], k_s[other]], axis=0),
            jnp.concatenate([v_s[one], v_s[other]], axis=0),
        )
        return carry

    lax.fori_loop(0, lax.div(count, 2), two, 0)

    @pl.when(lax.rem(count, 2) == 1)
    def _():
        arrive(count - 1)
        span = span_at(order, count - 1)
        block.fast(k_s[span], v_s[span])

    def rest(i, carry):
        arrive(i)
        return carry

    lax.fori_loop(count, SPANS, rest, 0)


def near_kernel(group, order, mask, q, ka, va, kb, vb, here, there, *refs):
    l_out, acc_out, q2, l, acc, q_s, k_s, v_s, ck_s, cv_s, q_sems, sems, cache_sems, out_sems = refs
    queries = Loads(lambda c: [(q.at[c], q_s.at[c])], q_sems)
    loads = span_loads(ka, va, kb, vb, k_s, v_s, sems)

    def cache_parts(x):
        rows = pl.ds(x * ROWS, ROWS)
        held, chip = (here, there)[x // 2], x % 2
        return [(held.at[2 * chip], ck_s.at[rows]), (held.at[2 * chip + 1], cv_s.at[rows])]

    cache = Loads(cache_parts, cache_sems)
    results = Loads(lambda c: [(l.at[c], l_out.at[c]), (acc.at[c], acc_out.at[c])], out_sems)
    queries.start(0)
    for x in range(SPANS):
        cache.start(x)
    queries.wait(0)
    for x in range(SPANS):
        cache.wait(x)
    for i in range(SPANS):
        loads.start(span_at(order, i))
    for c in range(1, SPANS):
        queries.start(c)

    def one_span(c, carry):
        @pl.when(c > 0)
        def _():
            queries.wait(c)

        block = Block(q2, l.at[c], acc.at[c])
        block.load(q_s[c])
        block.clear()
        seen = blocks_seen(group, mask, c)

        @pl.when(sum(seen) > 0)
        def _():
            block.fast(ck_s[...], cv_s[...], seen)

        over_spans(order, c, loads, block, k_s, v_s)
        results.start(c)
        return carry

    lax.fori_loop(0, SPANS, one_span, 0)
    for c in range(SPANS):
        results.wait(c)


def far_kernel(group, order, mask, q, *refs):
    spans = refs[:8]
    ka, va, kb, vb = spans[4:]
    here, there, l_in, acc_in, o_ref, q2, l, acc, q_s, k_s, v_s = refs[8:19]
    q_sems, sems, in_sems, m, k_x, v_x, x_sems = refs[19:]
    loads = span_loads(ka, va, kb, vb, k_s, v_s, sems)
    state = Loads(
        lambda c: [(q.at[c], q_s.at[c]), (l_in.at[c], l.at[c]), (acc_in.at[c], acc.at[c])], in_sems
    )
    state.start(0)
    loads.start(span_at(order, 0))
    state.wait(0)
    for i in range(1, SPANS):
        loads.start(span_at(order, i))
    for c in range(1, SPANS):
        state.start(c)

    def one_span(c, carry):
        count = order[c] + 1

        @pl.when(c > 0)
        def _():
            state.wait(c)

        block = Block(q2, l.at[c], acc.at[c])
        block.load(q_s[c])
        over_spans(order, c, loads, block, k_s, v_s)

        @pl.when(block.finish(o_ref.at[c]))
        def _():
            block.clear()
            m[...] = jnp.full(m.shape, LOW, jnp.float32)

            def fetch(k, v):
                piece = Loads(lambda _: [(k, k_x), (v, v_x)], x_sems)
                piece.start(0)
                piece.wait(0)

            def careful_step(i, carry):
                span = span_at(order, i)
                for quarter in range(4):
                    fetch(spans[2 * quarter].at[span], spans[2 * quarter + 1].at[span])
                    block.careful(m, k_x[...], v_x[...])
                return carry

            lax.fori_loop(0, count, careful_step, 0)
            seen = blocks_seen(group, mask, c)
            for x in range(SPANS):
                held, chip = (here, there)[x // 2], x % 2
                fetch(held.at[2 * chip], held.at[2 * chip + 1])
                for b in range(2):

                    @pl.when(seen[2 * x + b] > 0)
                    def _():
                        rows = slice(b * BLK, (b + 1) * BLK)
                        block.careful(m, k_x[rows, :], v_x[rows, :])

            block.finish(o_ref.at[c])

        return carry

    lax.fori_loop(0, SPANS, one_span, 0)


def call(kernel, name, scalars, arrays, outs, out_space, scratch, flops):
    return pl.pallas_call(
        kernel,
        grid_spec=pltpu.PrefetchScalarGridSpec(
            num_scalar_prefetch=len(scalars),
            grid=(),
            in_specs=[pl.BlockSpec(memory_space=pl.ANY)] * len(arrays),
            out_specs=[pl.BlockSpec(memory_space=out_space)] * len(outs),
            scratch_shapes=[pltpu.VMEM((ROWS, 2 * HD), jnp.bfloat16)] + scratch,
        ),
        out_shape=[jax.ShapeDtypeStruct((SPANS, ROWS, HD), dtype) for dtype in outs],
        compiler_params=pltpu.CompilerParams(vmem_limit_bytes=MEMORY),
        cost_estimate=pl.CostEstimate(
            flops=flops, bytes_accessed=12_000_000, transcendentals=20_000_000
        ),
        name=name,
    )(*scalars, *arrays)


def sems(*shape):
    return pltpu.SemaphoreType.DMA(shape)


STATE = [pltpu.VMEM((SPANS, ROWS, HD), jnp.float32)] * 2
QUERIES = [pltpu.VMEM((SPANS, ROWS, HD), jnp.bfloat16)]
SPAN_KEYS = [pltpu.VMEM((SPANS, 2 * ROWS, HD), jnp.bfloat16)] * 2
CACHE_KEYS = [pltpu.VMEM((SPAN_TOK, HD), jnp.bfloat16)] * 2
CAREFUL = [pltpu.VMEM((ROWS, HD), jnp.float32)] + [pltpu.VMEM((ROWS, HD), jnp.bfloat16)] * 2


def near(group, order, mask, q, spans, cached):
    return call(
        near_kernel, "near", [group, order, mask], [q, *spans, *cached],
        [jnp.float32] * 2, pl.ANY,
        STATE + QUERIES + SPAN_KEYS + CACHE_KEYS
        + [sems(SPANS, 1), sems(SPANS, 4), sems(SPANS, 2), sems(SPANS, 2)],
        29_000_000_000,
    )


def far(group, order, mask, q, spans, cached, state):
    return call(
        far_kernel, "far", [group, order, mask], [q, *spans, *cached, *state],
        [jnp.bfloat16], pltpu.VMEM,
        STATE + QUERIES + SPAN_KEYS + [sems(SPANS, 1), sems(SPANS, 4), sems(SPANS, 3)]
        + CAREFUL + [sems(1, 2)],
        17_000_000_000,
    )[0]


def on_device(
    queries, keys, values, cache_keys, cache_values, gate_table, noise_steps, span_order, block_mask
):
    group = jnp.reshape(lax.axis_index("span"), (1,)).astype(jnp.int32)
    apart = [lax.ppermute(x, "span", CHIP_SWAP) for x in (cache_keys, cache_values)]
    sent = pack(keys, values, queries).reshape(SPANS * H, 3 * PART, HD)
    sent, apart = lax.optimization_barrier((sent, apart))
    got = lax.all_to_all(sent, EVERYONE, 0, 0, tiled=True)
    cached = jnp.stack([cache_keys, cache_values, *apart])
    cached = [cached, lax.ppermute(cached, "span", CORE_SWAP)]
    k0, v0, q = (got[:, i * PART : (i + 1) * PART].reshape(SPANS, ROWS, HD) for i in range(3))
    k1, v1 = (lax.ppermute(x, "span", CORE_SWAP) for x in (k0, v0))
    k2, v2 = (lax.ppermute(x, "span", CHIP_SWAP) for x in (k0, v0))

    state = near(group, span_order, block_mask, q, [k0, v0, k1, v1], cached)
    k2, v2, state = lax.optimization_barrier((k2, v2, state))
    k3, v3 = (lax.ppermute(x, "span", CORE_SWAP) for x in (k2, v2))
    out = far(
        group, span_order, block_mask, q, [k0, v0, k1, v1, k2, v2, k3, v3], cached, state
    )
    out = lax.all_to_all(out.reshape(SPANS * H, PART, HD), EVERYONE, 0, 0, tiled=True)
    return apply_gate(group, noise_steps, out.reshape(SPANS, H, PART, HD), gate_table)


def solution(mesh):
    placed = (
        P("span", "cp", None),
        P("span", "cp", None),
        P("span", "cp", None),
        P("span", "cp"),
        P("span", "cp"),
        P(),
        P(),
        P(),
        P(),
    )
    return jax.shard_map(
        on_device, mesh=mesh, in_specs=placed, out_specs=P("span", "cp", None), check_vma=False
    )
```

time: 436 us -> 271 us (0.62)
  Pallas kernels: 0 us -> 181 us
  matrix products: 168 us -> 0 us
  other arithmetic: 95.2 us -> 1 us
  blocking collectives: 73.2 us -> 21.4 us
  between operations: 15 us -> 0.08 us
  local copies, waits for them, and re-layouts: 15.5 us -> 4.31 us
  waiting for transfers between devices: 52.2 us -> 45.2 us
    pallas_call x0 -> x4, Pallas kernels: none -> 181 us  [the longest x2 176 us: call(): pl.pallas_call(kernel, grid_spec=pltpu.PrefetchScalarGridSpec(num_scalar_...]
    dot_general x24 -> x0, matrix products: 168 us -> none  [the longest x12 88 us: one_block(): jnp.einsum('qhk,khd->qhd', weights.astype(jnp.bfloat16), piece_values, pr...]
    reduce_sum x18 -> x0, other arithmetic: 76.9 us -> none  [the longest x12 75 us: one_block(): total_block = total_block * rescale + jnp.sum(weights, axis=2)]
    all_gather x2 -> x0, waiting for transfers between devices: 38.7 us -> none  [the longest x1 38.7 us: on_device(): piece_values = lax.all_gather(head_values, 'span', axis=0, tiled=True)]
    all_gather x2 -> x0, blocking collectives: 30.7 us -> none  [the longest x1 18.1 us: on_device(): piece_keys = lax.all_gather(local_cache_keys, 'span', axis=0, tiled=True)]
    all_to_all x2 -> x1, blocking collectives: 42.5 us -> 21.4 us  [on_device(): lax.all_to_all(out.reshape(SPANS * H, PART, HD), EVERYONE, 0, 0, tiled=True)]
    all_to_all x2 -> x1, waiting for transfers between devices: 13.4 us -> 31.2 us  [on_device(): got = lax.all_to_all(sent, EVERYONE, 0, 0, tiled=True)]
    ppermute x0 -> x9, waiting for transfers between devices: none -> 14 us  [the longest x2 6.15 us: on_device(): lax.ppermute(x, 'span', CHIP_SWAP)]
  transfers between devices with their start and end apart: 4 -> 10, of which waited for: 2 -> 7; matrix products, arithmetic and copies ran while one was open for 2% -> 1% of each run, Pallas kernels for 0% -> 11%
where the time goes in v2:
time: 271 us; the launch traced here: 272 us
  Pallas kernels  181 us (67%)
  waiting for transfers between devices  45.2 us (17%)
  blocking collectives  21.4 us (8%)
  starting transfers between devices  18.6 us (7%)
  local copies, waits for them, and re-layouts  4.31 us (2%)
    pallas_call x2, Pallas kernels, call(): pl.pallas_call(kernel, grid_spec=pltpu.PrefetchScalarGridSpec(num_scalar_...  176 us
    all_to_all x1, waiting for transfers between devices, on_device(): got = lax.all_to_all(sent, EVERYONE, 0, 0, tiled=True)  31.2 us
    all_to_all x1, blocking collectives, on_device(): lax.all_to_all(out.reshape(SPANS * H, PART, HD), EVERYONE, 0, 0, tiled=True)  21.4 us
    all_to_all x1, starting transfers between devices, on_device(): got = lax.all_to_all(sent, EVERYONE, 0, 0, tiled=True)  11.1 us
    ppermute x2, waiting for transfers between devices, on_device(): lax.ppermute(x, 'span', CHIP_SWAP)  6.15 us
  transfers between devices with their start and end apart: 10, of which 7 were waited for; matrix products, arithmetic and copies ran while one was open for 1% of the time, Pallas kernels for 11%

profile of v2, /device:TPU:1, one launch (start us, length us, event | category | flops | bytes accessed | tf_op | source)
XLA Modules:
  0.0 271.8 jit_solution(2845028785540621675)
XLA Ops:
  0.0 2.5 collective-permute-start
  2.5 2.8 %pack.1 = bf16[4,32,72,128]{3,2,1,0:T(8,128)(2,1)} custom-call(bf16[1,96,4096]{2,1,0:T(8,128)(2,1)} %k_ref.1, bf16[1,96,4096]{2,1,0:T(8,128)(2,1)} %v_ref.1, bf16[1,96,4096]{2,1,0:T(8,128)(2,1)} %q_ref.1), custom_call_target="tpu_custom_call" | custom-call | tf_op jit(solution)/shard_map/pack/pallas_call | solution.py:41
  5.3 1.9 collective-permute-done
  7.3 4.2 %collective-permute-done.1 = bf16[768,128]{1,0:T(8,128)(2,1)S(1)} collective-permute-done((bf16[768,128]{1,0:T(8,128)(2,1)}, bf16[768,128]{1,0:T(8,128)(2,1)S(1)}, u32[]{:S(2)}, u32[]{:S(2)}) %collective-permute-start.1) | collective-permute-done | bytes 196640 | tf_op jit(solution)/shard_map/ppermute | solution.py:392
  11.5 11.1 %all-to-all-start = ((bf16[128,72,128]{2,1,0:T(8,128)(2,1)}), bf16[128,72,128]{2,1,0:T(8,128)(2,1)S(1)}, u32[]{:S(2)}, u32[]{:S(2)}) async-start(bf16[128,72,128]{2,1,0:T(8,128)(2,1)} %bitcast.11), calls=%async_computation | async-start | bytes 4718592 | tf_op jit(solution)/shard_map/all_to_all | solution.py:395
  22.6 1.0 pad_maximum_fusion.here.refs_8_
  23.6 1.1 collective-permute-start.6
  24.7 31.2 %all-to-all-done = bf16[128,72,128]{2,1,0:T(8,128)(2,1)S(1)} async-done(((bf16[128,72,128]{2,1,0:T(8,128)(2,1)}), bf16[128,72,128]{2,1,0:T(8,128)(2,1)S(1)}, u32[]{:S(2)}, u32[]{:S(2)}) %all-to-all-start) | async-done | bytes 2359328 | tf_op jit(solution)/shard_map/all_to_all | solution.py:395
  55.9 1.6 fusion
  57.5 1.2 collective-permute-start.2
  58.6 1.5 collective-permute-start.5
  60.1 1.7 collective-permute-done.2.kb.refs_2_
  61.9 0.9 copy-done.3
  62.7 0.4 copy-done.4
  63.1 28.4 %near.1 = (f32[4,768,128]{2,1,0:T(8,128)}, f32[4,768,128]{2,1,0:T(8,128)}) custom-call(s32[1]{0:T(128)} %bitcast.group, s32[4]{0:T(128)} %order.3, s32[4,8]{1,0:T(4,128)} %mask.3, bf16[4,768,128]{2,1,0:T(8,128)(2,1)} %bitcast.17, bf16[4,768,128]{2,1,0:T(8,128)(2,1)} %bitcast.3.ka.refs_0_, bf16[4,768,128]{2,1,0:T(8,128)(2,1)} %bitcast.15, ...), custom_call_target="tpu_custom_call" | custom-call | flops 28999999488 | bytes 12000000 | tf_op jit(solution)/shard_map/near/pallas_call | solution.py:339
  91.5 2.9 %collective-permute-done.5.refs_5_ = bf16[4,768,128]{2,1,0:T(8,128)(2,1)} collective-permute-done((bf16[4,768,128]{2,1,0:T(8,128)(2,1)S(1)}, bf16[4,768,128]{2,1,0:T(8,128)(2,1)}, u32[]{:S(2)}, u32[]{:S(2)}) %collective-permute-start.5) | collective-permute-done | bytes 786464 | tf_op jit(solution)/shard_map/ppermute | solution.py:400
  94.4 1.4 collective-permute-start.7
  95.8 3.0 %collective-permute-done.7.refs_6_ = bf16[4,768,128]{2,1,0:T(8,128)(2,1)S(1)} collective-permute-done((bf16[4,768,128]{2,1,0:T(8,128)(2,1)S(1)}, bf16[4,768,128]{2,1,0:T(8,128)(2,1)S(1)}, u32[]{:S(2)}, u32[]{:S(2)}) %collective-permute-start.7) | collective-permute-done | bytes 786464 | tf_op jit(solution)/shard_map/ppermute | solution.py:404
  98.8 0.2 collective-permute-done.8.refs_7_
  99.0 0.6 copy-done.6
  99.6 0.9 copy-done.7
  100.5 147.2 %far.1 = bf16[4,768,128]{2,1,0:T(8,128)(2,1)} custom-call(s32[1]{0:T(128)} %bitcast.group, s32[4]{0:T(128)} %order.3, s32[4,8]{1,0:T(4,128)} %mask.3, bf16[4,768,128]{2,1,0:T(8,128)(2,1)} %bitcast.18, bf16[4,768,128]{2,1,0:T(8,128)(2,1)} %bitcast.3.ka.refs_0_, bf16[4,768,128]{2,1,0:T(8,128)(2,1)} %bitcast.16, bf16[4,768,128]{2,1,0:T(8,128)(2,1)} %copy-done.3, ...), custom_call_target="tpu_custom_call" | custom-call | flops 16999999488 | bytes 12000000 | tf_op jit(solution)/shard_map/far/pallas_call | solution.py:339
  247.7 21.4 %all_to_all.10 = bf16[128,24,128]{2,1,0:T(8,128)(2,1)} all-to-all(bf16[128,24,128]{2,1,0:T(8,128)(2,1)} %bitcast.19), channel_id=1, replica_groups=mesh['span'=4,'cp'=32] {'span','cp'}, dimensions={0} | all-to-all | bytes 1572864 | tf_op jit(solution)/shard_map/all_to_all | solution.py:408
  269.1 2.7 gate.1
  (19 shorter events, 0.1 us)
Async XLA Ops:
  0.0 7.3 %collective-permute-start = (bf16[768,128]{1,0:T(8,128)(2,1)}, bf16[768,128]{1,0:T(8,128)(2,1)S(1)}, u32[]{:S(2)}, u32[]{:S(2)}) collective-permute-start(bf16[768,128]{1,0:T(8,128)(2,1)} %param.12), channel_id=1, source_target_pairs={{0,64},{64,0},{32,96},{96,32},{1,65},{65,1},{33,97},{97,33},{2,66}... | collective-permute-start | bytes 589832 | tf_op jit(solution)/shard_map/ppermute | solution.py:392
  2.5 9.0 %collective-permute-start.1 = (bf16[768,128]{1,0:T(8,128)(2,1)}, bf16[768,128]{1,0:T(8,128)(2,1)S(1)}, u32[]{:S(2)}, u32[]{:S(2)}) collective-permute-start(bf16[768,128]{1,0:T(8,128)(2,1)} %param.13), channel_id=1, source_target_pairs={{0,64},{64,0},{32,96},{96,32},{1,65},{65,1},{33,97},{97,33},{2,66}... | collective-permute-start | bytes 589832 | tf_op jit(solution)/shard_map/ppermute | solution.py:392
  11.5 11.1 %copy-start.1 = (bf16[768,128]{1,0:T(8,128)(2,1)S(1)}, bf16[768,128]{1,0:T(8,128)(2,1)}, u32[]{:S(2)}) copy-start(bf16[768,128]{1,0:T(8,128)(2,1)} %param.13) | copy-start | bytes 589828
  11.5 11.1 %copy-start.2 = (bf16[768,128]{1,0:T(8,128)(2,1)S(1)}, bf16[768,128]{1,0:T(8,128)(2,1)}, u32[]{:S(2)}) copy-start(bf16[768,128]{1,0:T(8,128)(2,1)} %param.12) | copy-start | bytes 589828
  11.5 44.4 %all-to-all-start = ((bf16[128,72,128]{2,1,0:T(8,128)(2,1)}), bf16[128,72,128]{2,1,0:T(8,128)(2,1)S(1)}, u32[]{:S(2)}, u32[]{:S(2)}) async-start(bf16[128,72,128]{2,1,0:T(8,128)(2,1)} %bitcast.11), calls=%async_computation | async-start | bytes 4718592 | tf_op jit(solution)/shard_map/all_to_all | solution.py:395
  23.6 36.5 %collective-permute-start.6 = (bf16[4,768,128]{2,1,0:T(8,128)(2,1)}, bf16[4,768,128]{2,1,0:T(8,128)(2,1)}, u32[]{:S(2)}, u32[]{:S(2)}) collective-permute-start(bf16[4,768,128]{2,1,0:T(8,128)(2,1)} %pad_maximum_fusion.here.refs_8_), channel_id=1, source_target_pairs={{0,32},{32,0},{64,96},{96,64},{1,33},{33,1},{65,97},{97,65},{2,34}... | collective-permute-start | bytes 2359304 | tf_op jit(solution)/shard_map/ppermute | solution.py:397
  57.5 4.4 %copy-start = (bf16[128,24,128]{2,1,0:T(8,128)(2,1)}, bf16[128,24,128]{2,1,0:T(8,128)(2,1)S(1)}, u32[]{:S(2)}) copy-start(bf16[128,24,128]{2,1,0:T(8,128)(2,1)S(1)} %get-tuple-element.23) | copy-start | bytes 2359300
  57.5 4.4 %collective-permute-start.2 = (bf16[4,768,128]{2,1,0:T(8,128)(2,1)}, bf16[4,768,128]{2,1,0:T(8,128)(2,1)S(1)}, u32[]{:S(2)}, u32[]{:S(2)}) collective-permute-start(bf16[4,768,128]{2,1,0:T(8,128)(2,1)} %bitcast.3.ka.refs_0_), channel_id=1, source_target_pairs={{0,32},{32,0},{64,96},{96,64},{1,33},{33,1},{65,97},{97,65},{2,34}... | collective-permute-start | bytes 2359304 | tf_op jit(solution)/shard_map/ppermute | solution.py:399
  58.6 3.2 %collective-permute-start.3 = (bf16[4,768,128]{2,1,0:T(8,128)(2,1)S(1)}, bf16[4,768,128]{2,1,0:T(8,128)(2,1)S(1)}, u32[]{:S(2)}, u32[]{:S(2)}) collective-permute-start(bf16[4,768,128]{2,1,0:T(8,128)(2,1)S(1)} %bitcast.13), channel_id=1, source_target_pairs={{0,32},{32,0},{64,96},{96,64},{1,33},{33,1},{65,97},{97,65},{2,34}... | collective-permute-start | bytes 2359304 | tf_op jit(solution)/shard_map/ppermute | solution.py:399
  58.6 32.9 %collective-permute-start.4 = (bf16[4,768,128]{2,1,0:T(8,128)(2,1)}, bf16[4,768,128]{2,1,0:T(8,128)(2,1)S(1)}, u32[]{:S(2)}, u32[]{:S(2)}) collective-permute-start(bf16[4,768,128]{2,1,0:T(8,128)(2,1)} %bitcast.3.ka.refs_0_), channel_id=1, source_target_pairs={{0,64},{64,0},{32,96},{96,32},{1,65},{65,1},{33,97},{97,33},{2,66}... | collective-permute-start | bytes 2359304 | tf_op jit(solution)/shard_map/ppermute | solution.py:400
  58.6 35.8 %collective-permute-start.5 = (bf16[4,768,128]{2,1,0:T(8,128)(2,1)S(1)}, bf16[4,768,128]{2,1,0:T(8,128)(2,1)}, u32[]{:S(2)}, u32[]{:S(2)}) collective-permute-start(bf16[4,768,128]{2,1,0:T(8,128)(2,1)S(1)} %bitcast.14), channel_id=1, source_target_pairs={{0,64},{64,0},{32,96},{96,32},{1,65},{65,1},{33,97},{97,33},{2,66}... | collective-permute-start | bytes 2359304 | tf_op jit(solution)/shard_map/ppermute | solution.py:400
  61.8 0.9 copy-start.3
  61.8 1.2 copy-start.4
  91.5 7.5 %copy-start.5 = (bf16[4,768,128]{2,1,0:T(8,128)(2,1)}, bf16[4,768,128]{2,1,0:T(8,128)(2,1)S(1)}, u32[]{:S(2)}) copy-start(bf16[4,768,128]{2,1,0:T(8,128)(2,1)S(1)} %collective-permute-done.4.refs_4_) | copy-start | bytes 2359300
  94.4 4.4 %collective-permute-start.7 = (bf16[4,768,128]{2,1,0:T(8,128)(2,1)S(1)}, bf16[4,768,128]{2,1,0:T(8,128)(2,1)S(1)}, u32[]{:S(2)}, u32[]{:S(2)}) collective-permute-start(bf16[4,768,128]{2,1,0:T(8,128)(2,1)S(1)} %collective-permute-done.4.refs_4_), channel_id=1, source_target_pairs={{0,32},{32,0},{64,96},{96,64},{1,33},{33,1},{65,97},{97,65},{2,34}... | collective-permute-start | bytes 2359304 | tf_op jit(solution)/shard_map/ppermute | solution.py:404
  95.8 3.2 %collective-permute-start.8 = (bf16[4,768,128]{2,1,0:T(8,128)(2,1)}, bf16[4,768,128]{2,1,0:T(8,128)(2,1)S(1)}, u32[]{:S(2)}, u32[]{:S(2)}) collective-permute-start(bf16[4,768,128]{2,1,0:T(8,128)(2,1)} %collective-permute-done.5.refs_5_), channel_id=1, source_target_pairs={{0,32},{32,0},{64,96},{96,64},{1,33},{33,1},{65,97},{97,65},{2,34}... | collective-permute-start | bytes 2359304 | tf_op jit(solution)/shard_map/ppermute | solution.py:404
  98.8 0.9 copy-start.6
  99.6 0.9 copy-start.7

commit v3 on v2

--- a/solution.py
+++ b/solution.py
@@ -173,15 +173,15 @@
             copy.wait()
 
 
-def span_loads(ka, va, kb, vb, k_s, v_s, sems):
+def span_loads(kv_a, kv_b, k_s, v_s, sems):
     low, high = pl.ds(0, ROWS), pl.ds(ROWS, ROWS)
 
     def group(span):
         return [
-            (ka.at[span], k_s.at[span, low]),
-            (kb.at[span], k_s.at[span, high]),
-            (va.at[span], v_s.at[span, low]),
-            (vb.at[span], v_s.at[span, high]),
+            (kv_a.at[0, span], k_s.at[span, low]),
+            (kv_b.at[0, span], k_s.at[span, high]),
+            (kv_a.at[1, span], v_s.at[span, low]),
+            (kv_b.at[1, span], v_s.at[span, high]),
         ]
 
     return Loads(group, sems)
@@ -225,10 +225,10 @@
     lax.fori_loop(count, SPANS, rest, 0)
 
 
-def near_kernel(group, order, mask, q, ka, va, kb, vb, here, there, *refs):
+def near_kernel(group, order, mask, q, kv_a, kv_b, here, there, *refs):
     l_out, acc_out, q2, l, acc, q_s, k_s, v_s, ck_s, cv_s, q_sems, sems, cache_sems, out_sems = refs
     queries = Loads(lambda c: [(q.at[c], q_s.at[c])], q_sems)
-    loads = span_loads(ka, va, kb, vb, k_s, v_s, sems)
+    loads = span_loads(kv_a, kv_b, k_s, v_s, sems)
 
     def cache_parts(x):
         rows = pl.ds(x * ROWS, ROWS)
@@ -272,11 +272,10 @@
 
 
 def far_kernel(group, order, mask, q, *refs):
-    spans = refs[:8]
-    ka, va, kb, vb = spans[4:]
-    here, there, l_in, acc_in, o_ref, q2, l, acc, q_s, k_s, v_s = refs[8:19]
-    q_sems, sems, in_sems, m, k_x, v_x, x_sems = refs[19:]
-    loads = span_loads(ka, va, kb, vb, k_s, v_s, sems)
+    spans = refs[:4]
+    here, there, l_in, acc_in, o_ref, q2, l, acc, q_s, k_s, v_s = refs[4:15]
+    sems, in_sems, m, k_x, v_x, x_sems = refs[15:]
+    loads = span_loads(spans[2], spans[3], k_s, v_s, sems)
     state = Loads(
         lambda c: [(q.at[c], q_s.at[c]), (l_in.at[c], l.at[c]), (acc_in.at[c], acc.at[c])], in_sems
     )
@@ -311,8 +310,8 @@
 
             def careful_step(i, carry):
                 span = span_at(order, i)
-                for quarter in range(4):
-                    fetch(spans[2 * quarter].at[span], spans[2 * quarter + 1].at[span])
+                for kv in spans:
+                    fetch(kv.at[0, span], kv.at[1, span])
                     block.careful(m, k_x[...], v_x[...])
                 return carry
 
@@ -379,7 +378,7 @@
     return call(
         far_kernel, "far", [group, order, mask], [q, *spans, *cached, *state],
         [jnp.bfloat16], pltpu.VMEM,
-        STATE + QUERIES + SPAN_KEYS + [sems(SPANS, 1), sems(SPANS, 4), sems(SPANS, 3)]
+        STATE + QUERIES + SPAN_KEYS + [sems(SPANS, 4), sems(SPANS, 3)]
         + CAREFUL + [sems(1, 2)],
         17_000_000_000,
     )[0]
@@ -391,20 +390,22 @@
     group = jnp.reshape(lax.axis_index("span"), (1,)).astype(jnp.int32)
     apart = [lax.ppermute(x, "span", CHIP_SWAP) for x in (cache_keys, cache_values)]
     sent = pack(keys, values, queries).reshape(SPANS * H, 3 * PART, HD)
-    sent, apart = lax.optimization_barrier((sent, apart))
+    sent, apart[0] = lax.optimization_barrier((sent, apart[0]))
     got = lax.all_to_all(sent, EVERYONE, 0, 0, tiled=True)
+    got, apart = lax.optimization_barrier((got, apart))
     cached = jnp.stack([cache_keys, cache_values, *apart])
     cached = [cached, lax.ppermute(cached, "span", CORE_SWAP)]
-    k0, v0, q = (got[:, i * PART : (i + 1) * PART].reshape(SPANS, ROWS, HD) for i in range(3))
-    k1, v1 = (lax.ppermute(x, "span", CORE_SWAP) for x in (k0, v0))
-    k2, v2 = (lax.ppermute(x, "span", CHIP_SWAP) for x in (k0, v0))
-
-    state = near(group, span_order, block_mask, q, [k0, v0, k1, v1], cached)
-    k2, v2, state = lax.optimization_barrier((k2, v2, state))
-    k3, v3 = (lax.ppermute(x, "span", CORE_SWAP) for x in (k2, v2))
-    out = far(
-        group, span_order, block_mask, q, [k0, v0, k1, v1, k2, v2, k3, v3], cached, state
-    )
+    kv0 = got[:, : 2 * PART].reshape(SPANS, H, 2, PART, HD).transpose(2, 0, 1, 3, 4)
+    kv0 = kv0.reshape(2, SPANS, ROWS, HD)
+    kv2 = lax.ppermute(kv0, "span", CHIP_SWAP)
+    kv1 = lax.ppermute(kv0, "span", CORE_SWAP)
+    got, kv1 = lax.optimization_barrier((got, kv1))
+    q = got[:, 2 * PART :].reshape(SPANS, ROWS, HD)
+
+    state = near(group, span_order, block_mask, q, [kv0, kv1], cached)
+    kv2, state = lax.optimization_barrier((kv2, state))
+    kv3 = lax.ppermute(kv2, "span", CORE_SWAP)
+    out = far(group, span_order, block_mask, q, [kv0, kv1, kv2, kv3], cached, state)
     out = lax.all_to_all(out.reshape(SPANS * H, PART, HD), EVERYONE, 0, 0, tiled=True)
     return apply_gate(group, noise_steps, out.reshape(SPANS, H, PART, HD), gate_table)
 

time: 271 us -> 276 us (1.018); the launches traced: 272 us -> 272 us
    all_to_all x1, waiting for transfers between devices: 31.2 us -> 1.94 us  [on_device(): got = lax.all_to_all(sent, EVERYONE, 0, 0, tiled=True)]
    ppermute x2, waiting for transfers between devices: 6.15 us -> 31.7 us  [on_device(): lax.ppermute(x, 'span', CHIP_SWAP)]
    ppermute x6 -> x3, waiting for transfers between devices: 7.85 us -> 9.72 us  [the longest x1 3.27 us: on_device(): kv2 = lax.ppermute(kv0, 'span', CHIP_SWAP)]
  transfers between devices with their start and end apart: 10 -> 7, of which waited for: 7 -> 6; matrix products, arithmetic and copies ran while one was open for 1% -> 0% of each run, Pallas kernels for 11% -> 11%
where the time goes in v3:
time: 276 us; the launch traced here: 272 us
  Pallas kernels  183 us (66%)
  waiting for transfers between devices  43.4 us (16%)
  blocking collectives  24.1 us (9%)
  starting transfers between devices  17.7 us (6%)
  local copies, waits for them, and re-layouts  3.72 us (1%)
    pallas_call x2, Pallas kernels, call(): pl.pallas_call(kernel, grid_spec=pltpu.PrefetchScalarGridSpec(num_scalar_...  178 us
    ppermute x2, waiting for transfers between devices, on_device(): lax.ppermute(x, 'span', CHIP_SWAP)  31.7 us
    all_to_all x1, blocking collectives, on_device(): lax.all_to_all(out.reshape(SPANS * H, PART, HD), EVERYONE, 0, 0, tiled=True)  24.1 us
    all_to_all x1, starting transfers between devices, on_device(): got = lax.all_to_all(sent, EVERYONE, 0, 0, tiled=True)  11.1 us
  transfers between devices with their start and end apart: 7, of which 6 were waited for; matrix products, arithmetic and copies ran while one was open for 0% of the time, Pallas kernels for 11%

profile of v3, /device:TPU:1, one launch (start us, length us, event | category | flops | bytes accessed | tf_op | source)
XLA Modules:
  0.0 272.3 jit_solution(409057314455789346)
XLA Ops:
  0.0 2.5 collective-permute-start
  2.5 2.9 %pack.1 = bf16[4,32,72,128]{3,2,1,0:T(8,128)(2,1)} custom-call(bf16[1,96,4096]{2,1,0:T(8,128)(2,1)} %k_ref.1, bf16[1,96,4096]{2,1,0:T(8,128)(2,1)} %v_ref.1, bf16[1,96,4096]{2,1,0:T(8,128)(2,1)} %q_ref.1), custom_call_target="tpu_custom_call" | custom-call | tf_op jit(solution)/shard_map/pack/pallas_call | solution.py:41
  5.3 2.0 collective-permute-done
  7.3 11.1 %all-to-all-start = ((bf16[128,72,128]{2,1,0:T(8,128)(2,1)}), bf16[128,72,128]{2,1,0:T(8,128)(2,1)S(1)}, u32[]{:S(2)}, u32[]{:S(2)}) async-start(bf16[128,72,128]{2,1,0:T(8,128)(2,1)} %bitcast.13), calls=%async_computation | async-start | bytes 4718592 | tf_op jit(solution)/shard_map/all_to_all | solution.py:394
  18.4 1.6 collective-permute-start.1
  20.0 29.8 %collective-permute-done.1 = bf16[768,128]{1,0:T(8,128)(2,1)S(1)} collective-permute-done((bf16[768,128]{1,0:T(8,128)(2,1)S(1)}, bf16[768,128]{1,0:T(8,128)(2,1)S(1)}, u32[]{:S(2)}, u32[]{:S(2)}) %collective-permute-start.1) | collective-permute-done | bytes 196640 | tf_op jit(solution)/shard_map/ppermute | solution.py:391
  49.7 1.9 all-to-all-done
  51.7 0.1 slice.6
  51.8 0.0 copy-start.2
  51.8 1.5 copy.10
  53.3 1.2 collective-permute-start.2
  54.4 0.1 pad_maximum_fusion.here.refs_4_
  54.6 0.1 collective-permute-start.4
  54.7 0.1 collective-permute-start.3
  54.8 3.2 %collective-permute-done.2.kv_b.refs_1_ = bf16[2,4,768,128]{3,2,1,0:T(8,128)(2,1)} collective-permute-done((bf16[2,4,768,128]{3,2,1,0:T(8,128)(2,1)}, bf16[2,4,768,128]{3,2,1,0:T(8,128)(2,1)}, u32[]{:S(2)}, u32[]{:S(2)}) %collective-permute-start.2) | collective-permute-done | bytes 1572896 | tf_op jit(solution)/shard_map/ppermute | solution.py:401
  58.0 1.0 slice.7
  58.9 28.4 %near.1 = (f32[4,768,128]{2,1,0:T(8,128)}, f32[4,768,128]{2,1,0:T(8,128)}) custom-call(s32[1]{0:T(128)} %bitcast.group, s32[4]{0:T(128)} %order.3, s32[4,8]{1,0:T(4,128)} %mask.3, bf16[4,768,128]{2,1,0:T(8,128)(2,1)} %bitcast.16, bf16[2,4,768,128]{3,2,1,0:T(8,128)(2,1)} %bitcast.4.kv_a.refs_0_, bf16[2,4,768,128]{3,2,1,0:T(8,128)(2,1)} %collective-permute-done.2.kv_b.refs_1_, ...), custom_call_target="tpu_custom_call" | custom-call | flops 28999999488 | bytes 12000000 | tf_op jit(solution)/shard_map/near/pallas_call | solution.py:338
  87.4 3.3 %collective-permute-done.3.refs_2_ = bf16[2,4,768,128]{3,2,1,0:T(8,128)(2,1)} collective-permute-done((bf16[2,4,768,128]{3,2,1,0:T(8,128)(2,1)}, bf16[2,4,768,128]{3,2,1,0:T(8,128)(2,1)}, u32[]{:S(2)}, u32[]{:S(2)}) %collective-permute-start.3) | collective-permute-done | bytes 1572896 | tf_op jit(solution)/shard_map/ppermute | solution.py:400
  90.6 1.2 collective-permute-start.5
  91.9 3.2 %collective-permute-done.5.refs_3_ = bf16[2,4,768,128]{3,2,1,0:T(8,128)(2,1)S(1)} collective-permute-done((bf16[2,4,768,128]{3,2,1,0:T(8,128)(2,1)}, bf16[2,4,768,128]{3,2,1,0:T(8,128)(2,1)S(1)}, u32[]{:S(2)}, u32[]{:S(2)}) %collective-permute-start.5) | collective-permute-done | bytes 1572896 | tf_op jit(solution)/shard_map/ppermute | solution.py:407
  95.1 1.2 copy-done.5
  96.3 149.3 %far.1 = bf16[4,768,128]{2,1,0:T(8,128)(2,1)} custom-call(s32[1]{0:T(128)} %bitcast.group, s32[4]{0:T(128)} %order.3, s32[4,8]{1,0:T(4,128)} %mask.3, bf16[4,768,128]{2,1,0:T(8,128)(2,1)} %bitcast.17, bf16[2,4,768,128]{3,2,1,0:T(8,128)(2,1)} %bitcast.4.kv_a.refs_0_, bf16[2,4,768,128]{3,2,1,0:T(8,128)(2,1)} %collective-permute-done.2.kv_b.refs_1_, ...), custom_call_target="tpu_custom_call" | custom-call | flops 16999999488 | bytes 12000000 | tf_op jit(solution)/shard_map/far/pallas_call | solution.py:338
  245.6 24.1 %all_to_all.10 = bf16[128,24,128]{2,1,0:T(8,128)(2,1)} all-to-all(bf16[128,24,128]{2,1,0:T(8,128)(2,1)} %bitcast.18), channel_id=1, replica_groups=mesh['span'=4,'cp'=32] {'span','cp'}, dimensions={0} | all-to-all | bytes 1572864 | tf_op jit(solution)/shard_map/all_to_all | solution.py:409
  269.6 2.7 gate.1
  (11 shorter events, 0.0 us)
Async XLA Ops:
  0.0 7.3 %collective-permute-start = (bf16[768,128]{1,0:T(8,128)(2,1)}, bf16[768,128]{1,0:T(8,128)(2,1)S(1)}, u32[]{:S(2)}, u32[]{:S(2)}) collective-permute-start(bf16[768,128]{1,0:T(8,128)(2,1)} %param.12), channel_id=1, source_target_pairs={{0,64},{64,0},{32,96},{96,32},{1,65},{65,1},{33,97},{97,33},{2,66}... | collective-permute-start | bytes 589832 | tf_op jit(solution)/shard_map/ppermute | solution.py:391
  7.3 11.1 %copy-start.1 = (bf16[768,128]{1,0:T(8,128)(2,1)S(1)}, bf16[768,128]{1,0:T(8,128)(2,1)}, u32[]{:S(2)}) copy-start(bf16[768,128]{1,0:T(8,128)(2,1)} %param.13) | copy-start | bytes 589828
  7.3 44.4 %all-to-all-start = ((bf16[128,72,128]{2,1,0:T(8,128)(2,1)}), bf16[128,72,128]{2,1,0:T(8,128)(2,1)S(1)}, u32[]{:S(2)}, u32[]{:S(2)}) async-start(bf16[128,72,128]{2,1,0:T(8,128)(2,1)} %bitcast.13), calls=%async_computation | async-start | bytes 4718592 | tf_op jit(solution)/shard_map/all_to_all | solution.py:394
  18.4 31.4 %collective-permute-start.1 = (bf16[768,128]{1,0:T(8,128)(2,1)S(1)}, bf16[768,128]{1,0:T(8,128)(2,1)S(1)}, u32[]{:S(2)}, u32[]{:S(2)}) collective-permute-start(bf16[768,128]{1,0:T(8,128)(2,1)S(1)} %copy-done.1), channel_id=1, source_target_pairs={{0,64},{64,0},{32,96},{96,32},{1,65},{65,1},{33,97},{97,33},{2,66}... | collective-permute-start | bytes 589832 | tf_op jit(solution)/shard_map/ppermute | solution.py:391
  49.7 2.0 copy-start.3
  51.8 2.6 copy-start.2
  51.8 2.6 copy-start.4
  53.3 4.7 %collective-permute-start.2 = (bf16[2,4,768,128]{3,2,1,0:T(8,128)(2,1)}, bf16[2,4,768,128]{3,2,1,0:T(8,128)(2,1)}, u32[]{:S(2)}, u32[]{:S(2)}) collective-permute-start(bf16[2,4,768,128]{3,2,1,0:T(8,128)(2,1)} %bitcast.4.kv_a.refs_0_), channel_id=1, source_target_pairs={{0,32},{32,0},{64,96},{96,64},{1,33},{33,1},{65,97},{97,65},{2,34}... | collective-permute-start | bytes 4718600 | tf_op jit(solution)/shard_map/ppermute | solution.py:401
  54.6 4.4 %copy-start = (bf16[4,768,128]{2,1,0:T(8,128)(2,1)}, bf16[4,768,128]{2,1,0:T(8,128)(2,1)S(1)}, u32[]{:S(2)}) copy-start(bf16[4,768,128]{2,1,0:T(8,128)(2,1)S(1)} %pad_maximum_fusion.here.refs_4_) | copy-start | bytes 2359300
  54.6 4.4 %collective-permute-start.4 = (bf16[4,768,128]{2,1,0:T(8,128)(2,1)S(1)}, bf16[4,768,128]{2,1,0:T(8,128)(2,1)}, u32[]{:S(2)}, u32[]{:S(2)}) collective-permute-start(bf16[4,768,128]{2,1,0:T(8,128)(2,1)S(1)} %pad_maximum_fusion.here.refs_4_), channel_id=1, source_target_pairs={{0,32},{32,0},{64,96},{96,64},{1,33},{33,1},{65,97},{97,65},{2,34}... | collective-permute-start | bytes 2359304 | tf_op jit(solution)/shard_map/ppermute | solution.py:397
  54.7 36.0 %collective-permute-start.3 = (bf16[2,4,768,128]{3,2,1,0:T(8,128)(2,1)}, bf16[2,4,768,128]{3,2,1,0:T(8,128)(2,1)}, u32[]{:S(2)}, u32[]{:S(2)}) collective-permute-start(bf16[2,4,768,128]{3,2,1,0:T(8,128)(2,1)} %bitcast.4.kv_a.refs_0_), channel_id=1, source_target_pairs={{0,64},{64,0},{32,96},{96,32},{1,65},{65,1},{33,97},{97,33},{2,66}... | collective-permute-start | bytes 4718600 | tf_op jit(solution)/shard_map/ppermute | solution.py:400
  90.6 4.5 %collective-permute-start.5 = (bf16[2,4,768,128]{3,2,1,0:T(8,128)(2,1)}, bf16[2,4,768,128]{3,2,1,0:T(8,128)(2,1)S(1)}, u32[]{:S(2)}, u32[]{:S(2)}) collective-permute-start(bf16[2,4,768,128]{3,2,1,0:T(8,128)(2,1)} %collective-permute-done.3.refs_2_), channel_id=1, source_target_pairs={{0,32},{32,0},{64,96},{96,64},{1,33},{33,1},{65,97},{97,65},{2,34}... | collective-permute-start | bytes 4718600 | tf_op jit(solution)/shard_map/ppermute | solution.py:407
  95.1 1.2 copy-start.5

commit v4 on v3

--- a/solution.py
+++ b/solution.py
@@ -273,14 +273,15 @@
 
 def far_kernel(group, order, mask, q, *refs):
     spans = refs[:4]
-    here, there, l_in, acc_in, o_ref, q2, l, acc, q_s, k_s, v_s = refs[4:15]
-    sems, in_sems, m, k_x, v_x, x_sems = refs[15:]
+    here, there, l_in, acc_in, o_out, q2, l, acc, q_s, k_s, v_s = refs[4:15]
+    sems, in_sems, m, k_x, v_x, x_sems, o_s, out_sems = refs[15:]
+    results = Loads(lambda c: [(o_s.at[c], o_out.at[c])], out_sems)
     loads = span_loads(spans[2], spans[3], k_s, v_s, sems)
     state = Loads(
         lambda c: [(q.at[c], q_s.at[c]), (l_in.at[c], l.at[c]), (acc_in.at[c], acc.at[c])], in_sems
     )
+    loads.start(span_at(order, 0))
     state.start(0)
-    loads.start(span_at(order, 0))
     state.wait(0)
     for i in range(1, SPANS):
         loads.start(span_at(order, i))
@@ -298,7 +299,7 @@
         block.load(q_s[c])
         over_spans(order, c, loads, block, k_s, v_s)
 
-        @pl.when(block.finish(o_ref.at[c]))
+        @pl.when(block.finish(o_s.at[c]))
         def _():
             block.clear()
             m[...] = jnp.full(m.shape, LOW, jnp.float32)
@@ -327,11 +328,14 @@
                         rows = slice(b * BLK, (b + 1) * BLK)
                         block.careful(m, k_x[rows, :], v_x[rows, :])
 
-            block.finish(o_ref.at[c])
-
+            block.finish(o_s.at[c])
+
+        results.start(c)
         return carry
 
     lax.fori_loop(0, SPANS, one_span, 0)
+    for c in range(SPANS):
+        results.wait(c)
 
 
 def call(kernel, name, scalars, arrays, outs, out_space, scratch, flops):
@@ -377,9 +381,9 @@
 def far(group, order, mask, q, spans, cached, state):
     return call(
         far_kernel, "far", [group, order, mask], [q, *spans, *cached, *state],
-        [jnp.bfloat16], pltpu.VMEM,
+        [jnp.bfloat16], pl.ANY,
         STATE + QUERIES + SPAN_KEYS + [sems(SPANS, 4), sems(SPANS, 3)]
-        + CAREFUL + [sems(1, 2)],
+        + CAREFUL + [sems(1, 2)] + QUERIES + [sems(SPANS, 1)],
         17_000_000_000,
     )[0]
 

time: 276 us -> 272 us (0.986); the launches traced: 272 us -> 272 us
  no operation moved by 1% of the time
where the time goes in v4:
time: 272 us
  Pallas kernels  183 us (67%)
  waiting for transfers between devices  43.4 us (16%)
  blocking collectives  24.1 us (9%)
  starting transfers between devices  17.7 us (7%)
  local copies, waits for them, and re-layouts  3.72 us (1%)
    pallas_call x2, Pallas kernels, call(): pl.pallas_call(kernel, grid_spec=pltpu.PrefetchScalarGridSpec(num_scalar_...  177 us
    ppermute x2, waiting for transfers between devices, on_device(): lax.ppermute(x, 'span', CHIP_SWAP)  31.7 us
    all_to_all x1, blocking collectives, on_device(): lax.all_to_all(out.reshape(SPANS * H, PART, HD), EVERYONE, 0, 0, tiled=True)  24.1 us
    all_to_all x1, starting transfers between devices, on_device(): got = lax.all_to_all(sent, EVERYONE, 0, 0, tiled=True)  11.1 us
  transfers between devices with their start and end apart: 7, of which 6 were waited for; matrix products, arithmetic and copies ran while one was open for 0% of the time, Pallas kernels for 11%

profile of v4, /device:TPU:1, one launch (start us, length us, event | category | flops | bytes accessed | tf_op | source)
XLA Modules:
  0.0 271.9 jit_solution(9310006740562152589)
XLA Ops:
  0.0 2.5 collective-permute-start
  2.5 2.9 %pack.1 = bf16[4,32,72,128]{3,2,1,0:T(8,128)(2,1)} custom-call(bf16[1,96,4096]{2,1,0:T(8,128)(2,1)} %k_ref.1, bf16[1,96,4096]{2,1,0:T(8,128)(2,1)} %v_ref.1, bf16[1,96,4096]{2,1,0:T(8,128)(2,1)} %q_ref.1), custom_call_target="tpu_custom_call" | custom-call | tf_op jit(solution)/shard_map/pack/pallas_call | solution.py:41
  5.3 2.0 collective-permute-done
  7.3 11.1 %all-to-all-start = ((bf16[128,72,128]{2,1,0:T(8,128)(2,1)}), bf16[128,72,128]{2,1,0:T(8,128)(2,1)S(1)}, u32[]{:S(2)}, u32[]{:S(2)}) async-start(bf16[128,72,128]{2,1,0:T(8,128)(2,1)} %bitcast.13), calls=%async_computation | async-start | bytes 4718592 | tf_op jit(solution)/shard_map/all_to_all | solution.py:398
  18.4 1.6 collective-permute-start.1
  20.0 29.8 %collective-permute-done.1 = bf16[768,128]{1,0:T(8,128)(2,1)S(1)} collective-permute-done((bf16[768,128]{1,0:T(8,128)(2,1)S(1)}, bf16[768,128]{1,0:T(8,128)(2,1)S(1)}, u32[]{:S(2)}, u32[]{:S(2)}) %collective-permute-start.1) | collective-permute-done | bytes 196640 | tf_op jit(solution)/shard_map/ppermute | solution.py:395
  49.7 1.9 all-to-all-done
  51.7 0.1 slice.6
  51.8 0.0 copy-start.2
  51.8 1.5 copy.10
  53.3 1.2 collective-permute-start.2
  54.4 0.1 pad_maximum_fusion.here.refs_4_
  54.6 0.1 collective-permute-start.4
  54.7 0.1 collective-permute-start.3
  54.8 3.2 %collective-permute-done.2.kv_b.refs_1_ = bf16[2,4,768,128]{3,2,1,0:T(8,128)(2,1)} collective-permute-done((bf16[2,4,768,128]{3,2,1,0:T(8,128)(2,1)}, bf16[2,4,768,128]{3,2,1,0:T(8,128)(2,1)}, u32[]{:S(2)}, u32[]{:S(2)}) %collective-permute-start.2) | collective-permute-done | bytes 1572896 | tf_op jit(solution)/shard_map/ppermute | solution.py:405
  58.0 1.0 slice.7
  58.9 28.4 %near.1 = (f32[4,768,128]{2,1,0:T(8,128)}, f32[4,768,128]{2,1,0:T(8,128)}) custom-call(s32[1]{0:T(128)} %bitcast.group, s32[4]{0:T(128)} %order.3, s32[4,8]{1,0:T(4,128)} %mask.3, bf16[4,768,128]{2,1,0:T(8,128)(2,1)} %bitcast.16, bf16[2,4,768,128]{3,2,1,0:T(8,128)(2,1)} %bitcast.4.kv_a.refs_0_, bf16[2,4,768,128]{3,2,1,0:T(8,128)(2,1)} %collective-permute-done.2.kv_b.refs_1_, ...), custom_call_target="tpu_custom_call" | custom-call | flops 28999999488 | bytes 12000000 | tf_op jit(solution)/shard_map/near/pallas_call | solution.py:342
  87.4 3.3 %collective-permute-done.3.refs_2_ = bf16[2,4,768,128]{3,2,1,0:T(8,128)(2,1)} collective-permute-done((bf16[2,4,768,128]{3,2,1,0:T(8,128)(2,1)}, bf16[2,4,768,128]{3,2,1,0:T(8,128)(2,1)}, u32[]{:S(2)}, u32[]{:S(2)}) %collective-permute-start.3) | collective-permute-done | bytes 1572896 | tf_op jit(solution)/shard_map/ppermute | solution.py:404
  90.6 1.2 collective-permute-start.5
  91.9 3.2 %collective-permute-done.5.refs_3_ = bf16[2,4,768,128]{3,2,1,0:T(8,128)(2,1)S(1)} collective-permute-done((bf16[2,4,768,128]{3,2,1,0:T(8,128)(2,1)}, bf16[2,4,768,128]{3,2,1,0:T(8,128)(2,1)S(1)}, u32[]{:S(2)}, u32[]{:S(2)}) %collective-permute-start.5) | collective-permute-done | bytes 1572896 | tf_op jit(solution)/shard_map/ppermute | solution.py:411
  95.1 1.2 copy-done.5
  96.3 148.8 %far.1 = bf16[4,768,128]{2,1,0:T(8,128)(2,1)} custom-call(s32[1]{0:T(128)} %bitcast.group, s32[4]{0:T(128)} %order.3, s32[4,8]{1,0:T(4,128)} %mask.3, bf16[4,768,128]{2,1,0:T(8,128)(2,1)} %bitcast.17, bf16[2,4,768,128]{3,2,1,0:T(8,128)(2,1)} %bitcast.4.kv_a.refs_0_, bf16[2,4,768,128]{3,2,1,0:T(8,128)(2,1)} %collective-permute-done.2.kv_b.refs_1_, ...), custom_call_target="tpu_custom_call" | custom-call | flops 16999999488 | bytes 12000000 | tf_op jit(solution)/shard_map/far/pallas_call | solution.py:342
  245.1 24.1 %all_to_all.10 = bf16[128,24,128]{2,1,0:T(8,128)(2,1)} all-to-all(bf16[128,24,128]{2,1,0:T(8,128)(2,1)} %bitcast.18), channel_id=1, replica_groups=mesh['span'=4,'cp'=32] {'span','cp'}, dimensions={0} | all-to-all | bytes 1572864 | tf_op jit(solution)/shard_map/all_to_all | solution.py:413
  269.2 2.7 gate.1
  (11 shorter events, 0.0 us)
Async XLA Ops:
  0.0 7.3 %collective-permute-start = (bf16[768,128]{1,0:T(8,128)(2,1)}, bf16[768,128]{1,0:T(8,128)(2,1)S(1)}, u32[]{:S(2)}, u32[]{:S(2)}) collective-permute-start(bf16[768,128]{1,0:T(8,128)(2,1)} %param.12), channel_id=1, source_target_pairs={{0,64},{64,0},{32,96},{96,32},{1,65},{65,1},{33,97},{97,33},{2,66}... | collective-permute-start | bytes 589832 | tf_op jit(solution)/shard_map/ppermute | solution.py:395
  7.3 11.1 %copy-start.1 = (bf16[768,128]{1,0:T(8,128)(2,1)S(1)}, bf16[768,128]{1,0:T(8,128)(2,1)}, u32[]{:S(2)}) copy-start(bf16[768,128]{1,0:T(8,128)(2,1)} %param.13) | copy-start | bytes 589828
  7.3 44.4 %all-to-all-start = ((bf16[128,72,128]{2,1,0:T(8,128)(2,1)}), bf16[128,72,128]{2,1,0:T(8,128)(2,1)S(1)}, u32[]{:S(2)}, u32[]{:S(2)}) async-start(bf16[128,72,128]{2,1,0:T(8,128)(2,1)} %bitcast.13), calls=%async_computation | async-start | bytes 4718592 | tf_op jit(solution)/shard_map/all_to_all | solution.py:398
  18.4 31.4 %collective-permute-start.1 = (bf16[768,128]{1,0:T(8,128)(2,1)S(1)}, bf16[768,128]{1,0:T(8,128)(2,1)S(1)}, u32[]{:S(2)}, u32[]{:S(2)}) collective-permute-start(bf16[768,128]{1,0:T(8,128)(2,1)S(1)} %copy-done.1), channel_id=1, source_target_pairs={{0,64},{64,0},{32,96},{96,32},{1,65},{65,1},{33,97},{97,33},{2,66}... | collective-permute-start | bytes 589832 | tf_op jit(solution)/shard_map/ppermute | solution.py:395
  49.7 2.0 copy-start.3
  51.8 2.6 copy-start.2
  51.8 2.6 copy-start.4
  53.3 4.7 %collective-permute-start.2 = (bf16[2,4,768,128]{3,2,1,0:T(8,128)(2,1)}, bf16[2,4,768,128]{3,2,1,0:T(8,128)(2,1)}, u32[]{:S(2)}, u32[]{:S(2)}) collective-permute-start(bf16[2,4,768,128]{3,2,1,0:T(8,128)(2,1)} %bitcast.4.kv_a.refs_0_), channel_id=1, source_target_pairs={{0,32},{32,0},{64,96},{96,64},{1,33},{33,1},{65,97},{97,65},{2,34}... | collective-permute-start | bytes 4718600 | tf_op jit(solution)/shard_map/ppermute | solution.py:405
  54.6 4.4 %copy-start = (bf16[4,768,128]{2,1,0:T(8,128)(2,1)}, bf16[4,768,128]{2,1,0:T(8,128)(2,1)S(1)}, u32[]{:S(2)}) copy-start(bf16[4,768,128]{2,1,0:T(8,128)(2,1)S(1)} %pad_maximum_fusion.here.refs_4_) | copy-start | bytes 2359300
  54.6 4.4 %collective-permute-start.4 = (bf16[4,768,128]{2,1,0:T(8,128)(2,1)S(1)}, bf16[4,768,128]{2,1,0:T(8,128)(2,1)}, u32[]{:S(2)}, u32[]{:S(2)}) collective-permute-start(bf16[4,768,128]{2,1,0:T(8,128)(2,1)S(1)} %pad_maximum_fusion.here.refs_4_), channel_id=1, source_target_pairs={{0,32},{32,0},{64,96},{96,64},{1,33},{33,1},{65,97},{97,65},{2,34}... | collective-permute-start | bytes 2359304 | tf_op jit(solution)/shard_map/ppermute | solution.py:401
  54.7 36.0 %collective-permute-start.3 = (bf16[2,4,768,128]{3,2,1,0:T(8,128)(2,1)}, bf16[2,4,768,128]{3,2,1,0:T(8,128)(2,1)}, u32[]{:S(2)}, u32[]{:S(2)}) collective-permute-start(bf16[2,4,768,128]{3,2,1,0:T(8,128)(2,1)} %bitcast.4.kv_a.refs_0_), channel_id=1, source_target_pairs={{0,64},{64,0},{32,96},{96,32},{1,65},{65,1},{33,97},{97,33},{2,66}... | collective-permute-start | bytes 4718600 | tf_op jit(solution)/shard_map/ppermute | solution.py:404
  90.6 4.5 %collective-permute-start.5 = (bf16[2,4,768,128]{3,2,1,0:T(8,128)(2,1)}, bf16[2,4,768,128]{3,2,1,0:T(8,128)(2,1)S(1)}, u32[]{:S(2)}, u32[]{:S(2)}) collective-permute-start(bf16[2,4,768,128]{3,2,1,0:T(8,128)(2,1)} %collective-permute-done.3.refs_2_), channel_id=1, source_target_pairs={{0,32},{32,0},{64,96},{96,64},{1,33},{33,1},{65,97},{97,65},{2,34}... | collective-permute-start | bytes 4718600 | tf_op jit(solution)/shard_map/ppermute | solution.py:411
  95.1 1.2 copy-start.5

commit v5 on v4

--- a/solution.py
+++ b/solution.py
@@ -394,7 +394,6 @@
     group = jnp.reshape(lax.axis_index("span"), (1,)).astype(jnp.int32)
     apart = [lax.ppermute(x, "span", CHIP_SWAP) for x in (cache_keys, cache_values)]
     sent = pack(keys, values, queries).reshape(SPANS * H, 3 * PART, HD)
-    sent, apart[0] = lax.optimization_barrier((sent, apart[0]))
     got = lax.all_to_all(sent, EVERYONE, 0, 0, tiled=True)
     got, apart = lax.optimization_barrier((got, apart))
     cached = jnp.stack([cache_keys, cache_values, *apart])

time: 272 us -> 273 us (level)
  transfers between devices with their start and end apart: 7 -> 7, of which waited for: 6 -> 5; matrix products, arithmetic and copies ran while one was open for 0% -> 0% of each run, Pallas kernels for 11% -> 10%
where the time goes in v5:
time: 273 us; the launch traced here: 271 us
  Pallas kernels  182 us (67%)
  waiting for transfers between devices  43.5 us (16%)
  blocking collectives  25.8 us (9%)
  starting transfers between devices  15.6 us (6%)
  local copies, waits for them, and re-layouts  4.3 us (2%)
    pallas_call x2, Pallas kernels, call(): pl.pallas_call(kernel, grid_spec=pltpu.PrefetchScalarGridSpec(num_scalar_...  176 us
    ppermute x2, waiting for transfers between devices, on_device(): lax.ppermute(x, 'span', CHIP_SWAP)  33.9 us
    all_to_all x1, blocking collectives, on_device(): lax.all_to_all(out.reshape(SPANS * H, PART, HD), EVERYONE, 0, 0, tiled=True)  25.8 us
    all_to_all x1, starting transfers between devices, on_device(): got = lax.all_to_all(sent, EVERYONE, 0, 0, tiled=True)  11.5 us
  transfers between devices with their start and end apart: 7, of which 5 were waited for; matrix products, arithmetic and copies ran while one was open for 0% of the time, Pallas kernels for 10%

profile of v5, /device:TPU:1, one launch (start us, length us, event | category | flops | bytes accessed | tf_op | source)
XLA Modules:
  0.0 271.4 jit_solution(15270651905847540696)
XLA Ops:
  0.0 2.9 %pack.1 = bf16[4,32,72,128]{3,2,1,0:T(8,128)(2,1)} custom-call(bf16[1,96,4096]{2,1,0:T(8,128)(2,1)} %k_ref.1, bf16[1,96,4096]{2,1,0:T(8,128)(2,1)} %v_ref.1, bf16[1,96,4096]{2,1,0:T(8,128)(2,1)} %q_ref.1), custom_call_target="tpu_custom_call" | custom-call | tf_op jit(solution)/shard_map/pack/pallas_call | solution.py:41
  2.9 11.5 %all-to-all-start = ((bf16[128,72,128]{2,1,0:T(8,128)(2,1)}), bf16[128,72,128]{2,1,0:T(8,128)(2,1)S(1)}, u32[]{:S(2)}, u32[]{:S(2)}) async-start(bf16[128,72,128]{2,1,0:T(8,128)(2,1)} %bitcast.13), calls=%async_computation | async-start | bytes 4718592 | tf_op jit(solution)/shard_map/all_to_all | solution.py:397
  14.4 1.6 collective-permute-start
  16.0 0.1 collective-permute-start.1
  16.1 29.7 %collective-permute-done = bf16[768,128]{1,0:T(8,128)(2,1)S(1)} collective-permute-done((bf16[768,128]{1,0:T(8,128)(2,1)S(1)}, bf16[768,128]{1,0:T(8,128)(2,1)S(1)}, u32[]{:S(2)}, u32[]{:S(2)}) %collective-permute-start) | collective-permute-done | bytes 196640 | tf_op jit(solution)/shard_map/ppermute | solution.py:395
  45.7 4.2 %collective-permute-done.1 = bf16[768,128]{1,0:T(8,128)(2,1)S(1)} collective-permute-done((bf16[768,128]{1,0:T(8,128)(2,1)S(1)}, bf16[768,128]{1,0:T(8,128)(2,1)S(1)}, u32[]{:S(2)}, u32[]{:S(2)}) %collective-permute-start.1) | collective-permute-done | bytes 196640 | tf_op jit(solution)/shard_map/ppermute | solution.py:395
  50.0 0.1 slice.6
  50.1 0.6 copy-done.5
  50.6 1.5 copy.10
  52.1 0.8 collective-permute-start.2
  52.9 0.1 pad_maximum_fusion.here.refs_4_
  53.0 0.1 collective-permute-start.4
  53.1 0.3 collective-permute-start.3
  53.4 3.0 %collective-permute-done.2.kv_b.refs_1_ = bf16[2,4,768,128]{3,2,1,0:T(8,128)(2,1)} collective-permute-done((bf16[2,4,768,128]{3,2,1,0:T(8,128)(2,1)}, bf16[2,4,768,128]{3,2,1,0:T(8,128)(2,1)}, u32[]{:S(2)}, u32[]{:S(2)}) %collective-permute-start.2) | collective-permute-done | bytes 1572896 | tf_op jit(solution)/shard_map/ppermute | solution.py:404
  56.4 1.0 slice.7
  57.4 0.0 collective-permute-done.4.there.refs_5_
  57.4 28.4 %near.1 = (f32[4,768,128]{2,1,0:T(8,128)}, f32[4,768,128]{2,1,0:T(8,128)}) custom-call(s32[1]{0:T(128)} %bitcast.group, s32[4]{0:T(128)} %order.3, s32[4,8]{1,0:T(4,128)} %mask.3, bf16[4,768,128]{2,1,0:T(8,128)(2,1)} %bitcast.16, bf16[2,4,768,128]{3,2,1,0:T(8,128)(2,1)} %bitcast.4.kv_a.refs_0_, bf16[2,4,768,128]{3,2,1,0:T(8,128)(2,1)} %collective-permute-done.2.kv_b.refs_1_, ...), custom_call_target="tpu_custom_call" | custom-call | flops 28999999488 | bytes 12000000 | tf_op jit(solution)/shard_map/near/pallas_call | solution.py:342
  85.8 3.3 %collective-permute-done.3.refs_2_ = bf16[2,4,768,128]{3,2,1,0:T(8,128)(2,1)} collective-permute-done((bf16[2,4,768,128]{3,2,1,0:T(8,128)(2,1)}, bf16[2,4,768,128]{3,2,1,0:T(8,128)(2,1)}, u32[]{:S(2)}, u32[]{:S(2)}) %collective-permute-start.3) | collective-permute-done | bytes 1572896 | tf_op jit(solution)/shard_map/ppermute | solution.py:403
  89.1 1.2 collective-permute-start.5
  90.3 3.2 %collective-permute-done.5.refs_3_ = bf16[2,4,768,128]{3,2,1,0:T(8,128)(2,1)S(1)} collective-permute-done((bf16[2,4,768,128]{3,2,1,0:T(8,128)(2,1)}, bf16[2,4,768,128]{3,2,1,0:T(8,128)(2,1)S(1)}, u32[]{:S(2)}, u32[]{:S(2)}) %collective-permute-start.5) | collective-permute-done | bytes 1572896 | tf_op jit(solution)/shard_map/ppermute | solution.py:410
  93.6 1.2 copy-done.7
  94.8 148.0 %far.1 = bf16[4,768,128]{2,1,0:T(8,128)(2,1)} custom-call(s32[1]{0:T(128)} %bitcast.group, s32[4]{0:T(128)} %order.3, s32[4,8]{1,0:T(4,128)} %mask.3, bf16[4,768,128]{2,1,0:T(8,128)(2,1)} %bitcast.17, bf16[2,4,768,128]{3,2,1,0:T(8,128)(2,1)} %bitcast.4.kv_a.refs_0_, bf16[2,4,768,128]{3,2,1,0:T(8,128)(2,1)} %collective-permute-done.2.kv_b.refs_1_, ...), custom_call_target="tpu_custom_call" | custom-call | flops 16999999488 | bytes 12000000 | tf_op jit(solution)/shard_map/far/pallas_call | solution.py:342
  242.8 25.8 %all_to_all.10 = bf16[128,24,128]{2,1,0:T(8,128)(2,1)} all-to-all(bf16[128,24,128]{2,1,0:T(8,128)(2,1)} %bitcast.18), channel_id=1, replica_groups=mesh['span'=4,'cp'=32] {'span','cp'}, dimensions={0} | all-to-all | bytes 1572864 | tf_op jit(solution)/shard_map/all_to_all | solution.py:412
  268.7 2.7 gate.1
  (15 shorter events, 0.0 us)
Async XLA Ops:
  2.9 11.5 %copy-start.2 = (bf16[768,128]{1,0:T(8,128)(2,1)S(1)}, bf16[768,128]{1,0:T(8,128)(2,1)}, u32[]{:S(2)}) copy-start(bf16[768,128]{1,0:T(8,128)(2,1)} %param.12) | copy-start | bytes 589828
  2.9 13.1 %copy-start.1 = (bf16[768,128]{1,0:T(8,128)(2,1)S(1)}, bf16[768,128]{1,0:T(8,128)(2,1)}, u32[]{:S(2)}) copy-start(bf16[768,128]{1,0:T(8,128)(2,1)} %param.13) | copy-start | bytes 589828
  2.9 47.1 %all-to-all-start = ((bf16[128,72,128]{2,1,0:T(8,128)(2,1)}), bf16[128,72,128]{2,1,0:T(8,128)(2,1)S(1)}, u32[]{:S(2)}, u32[]{:S(2)}) async-start(bf16[128,72,128]{2,1,0:T(8,128)(2,1)} %bitcast.13), calls=%async_computation | async-start | bytes 4718592 | tf_op jit(solution)/shard_map/all_to_all | solution.py:397
  14.4 31.4 %collective-permute-start = (bf16[768,128]{1,0:T(8,128)(2,1)S(1)}, bf16[768,128]{1,0:T(8,128)(2,1)S(1)}, u32[]{:S(2)}, u32[]{:S(2)}) collective-permute-start(bf16[768,128]{1,0:T(8,128)(2,1)S(1)} %copy-done.2), channel_id=1, source_target_pairs={{0,64},{64,0},{32,96},{96,32},{1,65},{65,1},{33,97},{97,33},{2,66}... | collective-permute-start | bytes 589832 | tf_op jit(solution)/shard_map/ppermute | solution.py:395
  16.0 34.0 %collective-permute-start.1 = (bf16[768,128]{1,0:T(8,128)(2,1)S(1)}, bf16[768,128]{1,0:T(8,128)(2,1)S(1)}, u32[]{:S(2)}, u32[]{:S(2)}) collective-permute-start(bf16[768,128]{1,0:T(8,128)(2,1)S(1)} %copy-done.1), channel_id=1, source_target_pairs={{0,64},{64,0},{32,96},{96,32},{1,65},{65,1},{33,97},{97,33},{2,66}... | collective-permute-start | bytes 589832 | tf_op jit(solution)/shard_map/ppermute | solution.py:395
  45.7 4.3 %copy-start.3 = (bf16[768,128]{1,0:T(8,128)(2,1)}, bf16[768,128]{1,0:T(8,128)(2,1)S(1)}, u32[]{:S(2)}) copy-start(bf16[768,128]{1,0:T(8,128)(2,1)S(1)} %collective-permute-done) | copy-start | bytes 589828
  50.0 0.7 copy-start.5
  50.6 2.3 copy-start.4
  50.6 2.3 copy-start.6
  52.1 4.3 %collective-permute-start.2 = (bf16[2,4,768,128]{3,2,1,0:T(8,128)(2,1)}, bf16[2,4,768,128]{3,2,1,0:T(8,128)(2,1)}, u32[]{:S(2)}, u32[]{:S(2)}) collective-permute-start(bf16[2,4,768,128]{3,2,1,0:T(8,128)(2,1)} %bitcast.4.kv_a.refs_0_), channel_id=1, source_target_pairs={{0,32},{32,0},{64,96},{96,64},{1,33},{33,1},{65,97},{97,65},{2,34}... | collective-permute-start | bytes 4718600 | tf_op jit(solution)/shard_map/ppermute | solution.py:404
  53.0 4.4 %copy-start = (bf16[4,768,128]{2,1,0:T(8,128)(2,1)}, bf16[4,768,128]{2,1,0:T(8,128)(2,1)S(1)}, u32[]{:S(2)}) copy-start(bf16[4,768,128]{2,1,0:T(8,128)(2,1)S(1)} %pad_maximum_fusion.here.refs_4_) | copy-start | bytes 2359300
  53.0 4.4 %collective-permute-start.4 = (bf16[4,768,128]{2,1,0:T(8,128)(2,1)S(1)}, bf16[4,768,128]{2,1,0:T(8,128)(2,1)}, u32[]{:S(2)}, u32[]{:S(2)}) collective-permute-start(bf16[4,768,128]{2,1,0:T(8,128)(2,1)S(1)} %pad_maximum_fusion.here.refs_4_), channel_id=1, source_target_pairs={{0,32},{32,0},{64,96},{96,64},{1,33},{33,1},{65,97},{97,65},{2,34}... | collective-permute-start | bytes 2359304 | tf_op jit(solution)/shard_map/ppermute | solution.py:400
  53.1 36.0 %collective-permute-start.3 = (bf16[2,4,768,128]{3,2,1,0:T(8,128)(2,1)}, bf16[2,4,768,128]{3,2,1,0:T(8,128)(2,1)}, u32[]{:S(2)}, u32[]{:S(2)}) collective-permute-start(bf16[2,4,768,128]{3,2,1,0:T(8,128)(2,1)} %bitcast.4.kv_a.refs_0_), channel_id=1, source_target_pairs={{0,64},{64,0},{32,96},{96,32},{1,65},{65,1},{33,97},{97,33},{2,66}... | collective-permute-start | bytes 4718600 | tf_op jit(solution)/shard_map/ppermute | solution.py:403
  89.1 4.5 %collective-permute-start.5 = (bf16[2,4,768,128]{3,2,1,0:T(8,128)(2,1)}, bf16[2,4,768,128]{3,2,1,0:T(8,128)(2,1)S(1)}, u32[]{:S(2)}, u32[]{:S(2)}) collective-permute-start(bf16[2,4,768,128]{3,2,1,0:T(8,128)(2,1)} %collective-permute-done.3.refs_2_), channel_id=1, source_target_pairs={{0,32},{32,0},{64,96},{96,64},{1,33},{33,1},{65,97},{97,65},{2,34}... | collective-permute-start | bytes 4718600 | tf_op jit(solution)/shard_map/ppermute | solution.py:410
  93.6 1.2 copy-start.7
